TPU v7x, 512 devices: a whole 4x8x8 slice. The times are simulated.
512 devices in a mesh: dp: 32 (over z, x), chan: 16 (over y, core).
Axes of the slice: x: 4, y: 8, z: 8, core: 2. Of those that a mesh axis runs over, the one named last changes fastest.
Arguments:
- spec_u: float32 [2, 32768, 4096], P(None, 'dp', 'chan'), may hold values from -60 to 60
- spec_g: float32 [2, 32768, 4096], P(None, 'dp', 'chan'), may hold values from -60 to 60
- decay_length: float32 [4096], P('chan'), may hold values from 32 to 32768
- w_first: float32 [33, 64], replicated, may hold values from -1 to 1
- w_second: float32 [64, 64], replicated, may hold values from -0.75 to 0.75
- w_out: float32 [64, 4096], P(None, 'chan'), may hold values from -0.75 to 0.75
- moments_first: float32 [2, 33, 64], replicated, may hold values from -0.006 to 0.006, as said below
- moments_second: float32 [2, 64, 64], replicated, may hold values from -0.006 to 0.006, as said below
- moments_out: float32 [2, 64, 4096], P(None, None, 'chan'), may hold values from -0.006 to 0.006, as said below
Outputs:
- step_first: float32 [33, 64], replicated
- step_second: float32 [64, 64], replicated
- step_out: float32 [64, 4096], P(None, 'chan')
Inputs may be any that keep to these rules, and one draw needn't show every extreme that they name: `moments_first`: entry 0 is the first moment, entry 1 the second moment, which is positive. `moments_second`: entry 0 is the first moment, entry 1 the second moment, which is positive. `moments_out`: entry 0 is the first moment, entry 1 the second moment, which is positive.
All inputs are finite; a program needn't handle non-finite values.
Results may differ from a plain program's by a relative error of at most 0.00025.
Values sent between devices are 32-bit elements; how exact they have to be, the bound alone decides.
A program may use at most 64 MiB of HBM per device.

v0:
```python
import math

import jax
import jax.numpy as jnp
from jax import lax
from jax.sharding import PartitionSpec as P

BANDS = 16


beta_one = 0.9
beta_two = 0.999
adam_count = 10.0
adam_eps = 1e-08
weight_decay = 0.1
clip_norm = 1.0


def features(positions, length):
    bands = jnp.arange(1, BANDS + 1, dtype=jnp.int32)
    phase = bands[:, None] * positions[None, :] % length
    angle = 2.0 * math.pi / length * phase.astype(jnp.float32)
    first = (positions.astype(jnp.float32) / length)[None, :]
    return jnp.concatenate([first, jnp.cos(angle), jnp.sin(angle)], axis=0)


def adam_step(grad, weight, moments, scale):
    g = grad * scale
    first = beta_one * moments[0] + (1.0 - beta_one) * g
    second = beta_two * moments[1] + (1.0 - beta_two) * g * g
    first_hat = first / (1.0 - beta_one**adam_count)
    second_hat = second / (1.0 - beta_two**adam_count)
    return first_hat / (jnp.sqrt(second_hat) + adam_eps) + weight_decay * weight


def tables(rows, cols, modulus):
    phase = (
        jnp.arange(rows, dtype=jnp.int32)[:, None]
        * jnp.arange(cols, dtype=jnp.int32)[None, :]
        % modulus
    )
    angle = 2.0 * math.pi / modulus * phase.astype(jnp.float32)
    return (jnp.cos(angle), jnp.sin(angle))


def to_positions(spectrum, residue, cos_table, sin_table, freqs):
    highest = lax.Precision.HIGHEST
    width = spectrum.shape[1]
    phase = jnp.arange(width, dtype=jnp.int32) * residue % freqs
    angle = (2.0 * math.pi / freqs * phase.astype(jnp.float32))[:, None]
    twist_re = spectrum[0] * jnp.cos(angle) - spectrum[1] * jnp.sin(angle)
    twist_im = spectrum[0] * jnp.sin(angle) + spectrum[1] * jnp.cos(angle)
    values = jnp.dot(cos_table, twist_re, precision=highest) - jnp.dot(
        sin_table, twist_im, precision=highest
    )
    return values / freqs


def local(
    spec_u,
    spec_g,
    decay_length,
    w_first,
    w_second,
    w_out,
    moments_first,
    moments_second,
    moments_out,
):
    highest = lax.Precision.HIGHEST
    groups = lax.axis_size("dp")
    device = lax.axis_index("dp")
    width = spec_u.shape[1]
    freqs = width * groups
    length = freqs // 2
    half = width // 2
    prod_re = spec_g[0] * spec_u[0] + spec_g[1] * spec_u[1]
    prod_im = spec_g[1] * spec_u[0] - spec_g[0] * spec_u[1]
    spectrum = jnp.stack([prod_re, prod_im])
    cos_table, sin_table = tables(half, width, width)
    cos_small, sin_small = tables(groups, groups, groups)
    block = lax.all_to_all(spectrum[:, None], "dp", split_axis=2, concat_axis=1, tiled=True)
    real_part = jnp.einsum("up,pkc->ukc", cos_small, block[0], precision=highest) - jnp.einsum(
        "up,pkc->ukc", sin_small, block[1], precision=highest
    )
    imag_part = jnp.einsum("up,pkc->ukc", sin_small, block[0], precision=highest) + jnp.einsum(
        "up,pkc->ukc", cos_small, block[1], precision=highest
    )
    returned = lax.all_to_all(
        jnp.stack([real_part, imag_part]), "dp", split_axis=1, concat_axis=2, tiled=True
    )
    filter_grad = to_positions(returned[:, 0], device, cos_table, sin_table, freqs)
    positions = device + groups * jnp.arange(half, dtype=jnp.int32)
    feats = features(positions, length)
    pre_one = jnp.dot(w_first.T, feats, precision=highest)
    act_one = jnp.sin(pre_one)
    pre_two = jnp.dot(w_second.T, act_one, precision=highest)
    act_two = jnp.sin(pre_two)
    window = jnp.exp(-positions.astype(jnp.float32)[:, None] / decay_length[None, :])
    out_grad = filter_grad * window
    grad_out = jnp.dot(act_two, out_grad, precision=highest)
    hidden_part = jnp.dot(w_out, out_grad.T, precision=highest)
    upstream = lax.psum(hidden_part, "chan")
    back_two = upstream * jnp.cos(pre_two)
    grad_second = jnp.dot(act_one, back_two.T, precision=highest)
    back_one = jnp.dot(w_second, back_two, precision=highest) * jnp.cos(pre_one)
    grad_first = jnp.dot(feats, back_one.T, precision=highest)
    part_first = grad_first
    part_second = grad_second
    grad_first, grad_second, grad_out = lax.psum((part_first, part_second, grad_out), "dp")
    out_squares = lax.psum(jnp.sum(grad_out * grad_out), "chan")
    total = jnp.sum(grad_first * grad_first) + jnp.sum(grad_second * grad_second) + out_squares
    scale = jnp.minimum(1.0, clip_norm / (jnp.sqrt(total) + 1e-06))
    step_first = adam_step(grad_first, w_first, moments_first, scale)
    step_second = adam_step(grad_second, w_second, moments_second, scale)
    step_out = adam_step(grad_out, w_out, moments_out, scale)
    return (step_first, step_second, step_out)


def solution(mesh):
    return jax.shard_map(
        local,
        mesh=mesh,
        in_specs=(
            P(None, "dp", "chan"),
            P(None, "dp", "chan"),
            P("chan"),
            P(),
            P(),
            P(None, "chan"),
            P(),
            P(),
            P(None, None, "chan"),
        ),
        out_specs=(P(), P(), P(None, "chan")),
        check_vma=False,
    )
```

profile of v0, /device:TPU:24, one launch (start us, length us, event | category | flops | bytes accessed | tf_op | source)
XLA Modules:
  0.0 596.4 jit_solution(8434342586374053540)
XLA Ops:
  7.2 2.5 fusion.117
  9.7 8.6 %multiply_add_fusion = (f32[1,1024,256]{2,0,1:T(1,128)S(1)}, f32[1,1024,256]{2,0,1:T(1,128)S(1)}) fusion(f32[1,1024,256]{2,1,0:T(8,128)S(1)} %get-tuple-element.25, f32[1,1024,256]{2,1,0:T(8,128)S(1)} %get-tuple-element.14, f32[1,1024,256]{2,1,0:T(8,128)S(1)} %get-tuple-element.26, f32[1,1024,256]{2,1,0:T(8,128)S(1)} %get-tuple-element.13), kind=kLoop, calls=%fused_computation.31 | loop fusion | flops 1572864 | bytes 6291456 | tf_op jit(solution)/shard_map/add | solution.py:77
  18.2 1.9 pad_maximum_fusion
  20.1 1.4 broadcast_in_dim.2
  21.6 63.5 %all_to_all.8 = f32[2,1,1024,256]{3,1,0,2:T(1,128)S(1)} all-to-all(f32[2,1,1024,256]{3,1,0,2:T(1,128)S(1)} %broadcast_in_dim.2), channel_id=1, replica_groups=mesh['dp'=32,'chan'=16] {'dp'}, dimensions={2} | all-to-all | bytes 4194304 | tf_op jit(solution)/shard_map/all_to_all | solution.py:82
  85.1 1.4 fusion.116
  86.5 0.1 copy.42
  86.6 1.6 fusion.29
  88.2 1.6 fusion.27
  89.8 0.1 copy.43
  89.9 1.6 fusion.11
  91.5 1.6 fusion.10
  93.1 0.2 pad_maximum_fusion.1
  93.4 2.6 copy.33
  95.9 0.0 copy-start.3
  95.9 0.0 copy-start
  95.9 5.7 all-to-all-start.1
  101.6 0.0 all-reduce.6.cloned.1.call-start
  101.7 0.1 fusion.87
  101.8 0.2 fusion.73
  102.0 0.0 copy-done.3
  102.0 0.7 fusion.120
  102.8 0.0 copy-done
  102.8 0.3 fusion.121
  103.1 47.6 %all-to-all-done.1 = f32[2,32,32,256]{3,2,0,1:T(8,128)S(1)} async-done(((f32[2,32,32,256]{3,2,0,1:T(8,128)}), f32[2,32,32,256]{3,2,0,1:T(8,128)S(1)}, u32[]{:S(2)}, u32[]{:S(2)}) %all-to-all-start.1) | async-done | bytes 2097184 | tf_op jit(solution)/shard_map/all_to_all | solution.py:89
  150.7 0.1 fusion.115
  150.9 0.3 fusion.21
  151.2 0.0 copy-start.6
  151.2 13.4 %fusion.3 = f32[512,256]{1,0:T(8,128)S(1)} fusion(f32[1024,256]{1,0:T(8,128)S(1)} %get-tuple-element.8), kind=kOutput, calls=%fused_computation.8 | convolution fusion | flops 1617952768 | bytes 1572864 | tf_op jit(solution)/shard_map/dot_general | solution.py:53
  164.6 0.0 copy-done.6
  164.6 0.0 copy-start.1
  164.6 0.0 copy-start.5
  164.6 9.5 %fusion.18 = f32[512,256]{1,0:T(8,128)S(1)} fusion(f32[512,256]{1,0:T(8,128)S(1)} %fusion.3, f32[1024,256]{1,0:T(8,128)S(1)} %get-tuple-element.7, f32[256]{0:T(256)S(1)} %copy-done.6, f32[512]{0:T(512)S(1)} %convert_negate_fusion), kind=kOutput, calls=%fused_computation.21 | convolution fusion | flops 1618477056 | bytes 2100224 | tf_op jit(solution)/shard_map/dot_general | solution.py:53
  174.1 0.0 copy-start.4
  174.1 0.0 copy-start.2
  174.1 1.5 fusion.31
  175.6 0.0 all-reduce.6.cloned.1.call-update
  175.6 0.0 all-reduce.4.cloned.1.call-start
  175.7 0.0 copy-done.1
  175.7 1.3 convolution_bitcast_fusion
  177.0 0.0 all-reduce.4.cloned.1.call-update
  177.0 146.6 %all-reduce.6.cloned.1.call-done = f32[64,256]{1,0:T(8,128)} async-done(((f32[64,256]{1,0:T(8,128)}), f32[64,256]{1,0:T(8,128)}) %all-reduce.6.cloned.1.call-update) | async-done | bytes 65552 | tf_op jit(solution)/shard_map/psum | solution.py:110
  323.6 1.5 multiply_reduce_fusion
  325.0 0.0 copy-done.5
  325.1 22.9 %psum.39 = f32[]{:T(128)} all-reduce(f32[]{:T(128)} %multiply_reduce_fusion), channel_id=1, replica_groups=mesh['dp'=32,'chan'=16] {'chan'}, use_global_device_ids=true, to_apply=%region_7.8 | all-reduce | flops 1 | bytes 8 | tf_op jit(solution)/shard_map/psum | solution.py:111
  348.0 88.0 %all-reduce.4.cloned.1.call-done = f32[64,512]{1,0:T(8,128)} async-done(((f32[64,512]{1,0:T(8,128)}), f32[64,512]{1,0:T(8,128)}) %all-reduce.4.cloned.1.call-update) | async-done | bytes 131088 | tf_op jit(solution)/shard_map/psum | solution.py:103
  436.0 1.9 convolution_multiply_fusion
  437.9 0.2 fusion.40
  438.2 1.6 fusion.42
  439.8 143.8 %all-reduce = (f32[33,64]{1,0:T(8,128)S(1)}, f32[64,64]{1,0:T(8,128)S(1)}) all-reduce(f32[33,64]{1,0:T(8,128)S(1)} %fusion.40, f32[64,64]{1,0:T(8,128)S(1)} %fusion.42), channel_id=1, replica_groups=mesh['dp'=32,'chan'=16] {'dp'}, use_global_device_ids=true, to_apply=%region_1.2 | all-reduce | flops 6208 | bytes 49664 | tf_op jit(solution)/shard_map/psum | solution.py:110
  583.5 0.6 multiply_reduce_fusion.1
  584.1 0.6 multiply_reduce_fusion.2
  586.7 0.0 copy-done.4
  586.8 0.7 fusion.50
  587.4 0.6 fusion.58
  588.0 0.0 copy-done.2
  588.0 1.5 fusion.38
  (5 shorter events, 0.1 us)
Async XLA Ops:
  95.9 6.1 %copy-start.3 = (f32[33,64]{1,0:T(8,128)S(1)}, f32[33,64]{1,0:T(8,128)}, u32[]{:S(2)}) copy-start(f32[33,64]{1,0:T(8,128)} %param.12) | copy-start | bytes 25348
  95.9 6.8 %copy-start = (f32[64,64]{1,0:T(8,128)S(1)}, f32[64,64]{1,0:T(8,128)}, u32[]{:S(2)}) copy-start(f32[64,64]{1,0:T(8,128)} %param.13) | copy-start | bytes 49156
  95.9 54.8 %all-to-all-start.1 = ((f32[2,32,32,256]{3,2,0,1:T(8,128)}), f32[2,32,32,256]{3,2,0,1:T(8,128)S(1)}, u32[]{:S(2)}, u32[]{:S(2)}) async-start(f32[2,32,32,256]{3,2,0,1:T(8,128)} %copy.33), calls=%async_computation.1 | async-start | bytes 4194304 | tf_op jit(solution)/shard_map/all_to_all | solution.py:89
  101.6 221.9 %all-reduce.6.cloned.1.call-start = ((), (), s32[]{:S(2)}) async-start(), calls=%async_computation.3 | async-start | bytes 131072 | tf_op jit(solution)/shard_map/psum | solution.py:110
  151.2 13.4 %copy-start.6 = (f32[256]{0:T(256)S(1)}, f32[256]{0:T(256)}, u32[]{:S(2)}) copy-start(f32[256]{0:T(256)} %param.11) | copy-start | bytes 3076
  164.6 11.0 %copy-start.1 = (f32[64,256]{1,0:T(8,128)S(1)}, f32[64,256]{1,0:T(8,128)}, u32[]{:S(2)}) copy-start(f32[64,256]{1,0:T(8,128)} %param.14) | copy-start | bytes 196612
  164.6 160.4 %copy-start.5 = (f32[2,33,64]{2,0,1:T(2,128)S(1)}, f32[2,33,64]{2,0,1:T(2,128)}, u32[]{:S(2)}) copy-start(f32[2,33,64]{2,0,1:T(2,128)} %param.15) | copy-start | bytes 50692
  174.1 412.6 %copy-start.4 = (f32[2,64,64]{2,1,0:T(8,128)S(1)}, f32[2,64,64]{2,1,0:T(8,128)}, u32[]{:S(2)}) copy-start(f32[2,64,64]{2,1,0:T(8,128)} %param.16) | copy-start | bytes 98308
  174.1 413.9 %copy-start.2 = (f32[2,64,256]{2,1,0:T(8,128)S(1)}, f32[2,64,256]{2,1,0:T(8,128)}, u32[]{:S(2)}) copy-start(f32[2,64,256]{2,1,0:T(8,128)} %param.17) | copy-start | bytes 393220
  175.6 260.4 %all-reduce.4.cloned.1.call-start = ((), (), s32[]{:S(2)}) async-start(), calls=%async_computation.2 | async-start | bytes 262144 | tf_op jit(solution)/shard_map/psum | solution.py:103
Sparse Core Ops, SparseCore 0:
  175.7 147.7 all-reduce.5
  325.9 110.0 all-reduce.3
where the time goes:
time: 597 us; the launch traced here: 596 us
  waiting for transfers between devices  282 us (47%)
  blocking collectives  230 us (39%)
  matrix products  36.8 us (6%)
  other arithmetic  16.8 us (3%)
  between operations  16.4 us (3%)
  local copies, waits for them, and re-layouts  8.26 us (1%)
    psum x1, waiting for transfers between devices, local(): lax.psum((part_first, part_second, grad_out), 'dp')  147 us
    psum x1, blocking collectives, local(): lax.psum((part_first, part_second, grad_out), 'dp')  144 us
    psum x1, waiting for transfers between devices, local(): upstream = lax.psum(hidden_part, 'chan')  88 us
    all_to_all x1, blocking collectives, local(): lax.all_to_all(spectrum[:, None], 'dp', split_axis=2, concat_axis=1, tile...  63.5 us
    all_to_all x1, waiting for transfers between devices, local(): lax.all_to_all(jnp.stack([real_part, imag_part]), 'dp', split_axis=1, con...  47.6 us
    psum x1, blocking collectives, local(): out_squares = lax.psum(jnp.sum(grad_out * grad_out), 'chan')  22.9 us
    dot_general x1, matrix products, to_positions(): jnp.dot(sin_table, twist_im, precision=highest)  13.4 us
  transfers between devices with their start and end apart: 3, of which 3 were waited for; matrix products, arithmetic and copies ran while one was open for 1% of the time, Pallas kernels for 0%

commit v1 on v0

v1 whole, which is shorter than its diff:
```python
import functools
import math

import jax
import jax.numpy as jnp
import numpy as np
from jax import lax
from jax.experimental import pallas as pl
from jax.experimental.pallas import tpu as pltpu
from jax.sharding import PartitionSpec as P

MESH = pl.DeviceIdType.MESH
HIGHEST = lax.Precision.HIGHEST

BANDS = 16
HID = 64
DP = 32
CHAN = 16
FREQS = 32768
SEQ = 16384
ROWS = 1024
COLS = 256

beta_one = 0.9
beta_two = 0.999
adam_count = 10.0
adam_eps = 1e-08
weight_decay = 0.1
clip_norm = 1.0


def adam_step(grad, weight, first, second, scale):
    g = grad * scale
    first = beta_one * first + (1.0 - beta_one) * g
    second = beta_two * second + (1.0 - beta_two) * g * g
    first_hat = first / (1.0 - beta_one**adam_count)
    second_hat = second / (1.0 - beta_two**adam_count)
    return first_hat / (jnp.sqrt(second_hat) + adam_eps) + weight_decay * weight


def split(x):
    high = x.astype(jnp.bfloat16)
    low = (x - high.astype(jnp.float32)).astype(jnp.bfloat16)
    return high, low


def dot3(a, b, dims):
    def one(x, y):
        return lax.dot_general(x, y, (dims, ((), ())), preferred_element_type=jnp.float32)

    return one(a[0], b[0]) + one(a[0], b[1]) + one(a[1], b[0])


NN = ((1,), (0,))
NT = ((1,), (1,))


def times(z, angle_num, angle_den):
    re, im = z
    k = angle_num % angle_den
    if k == 0:
        return re, im
    if 4 * k == angle_den:
        return -im, re
    if 2 * k == angle_den:
        return -re, -im
    if 4 * k == 3 * angle_den:
        return im, -re
    if 8 * k == angle_den:
        r = math.sqrt(0.5)
        return (re - im) * r, (re + im) * r
    if 8 * k == 3 * angle_den:
        r = math.sqrt(0.5)
        return (re + im) * (-r), (re - im) * r
    c, s = math.cos(2 * math.pi * k / angle_den), math.sin(2 * math.pi * k / angle_den)
    return re * c - im * s, re * s + im * c


def dft(values):
    n = len(values)
    if n == 1:
        return values
    even, odd = dft(values[0::2]), dft(values[1::2])
    low, high = [], []
    for k in range(n // 2):
        t = times(odd[k], k, n)
        low.append((even[k][0] + t[0], even[k][1] + t[1]))
        high.append((even[k][0] - t[0], even[k][1] - t[1]))
    return low + high


def constants():
    lane = np.arange(256)[:, None] * np.arange(128)[None, :] % 256
    angle = 2.0 * np.pi / 256 * lane
    table = np.concatenate([np.cos(angle), -np.sin(angle)], axis=0).astype(np.float32)
    high = table.astype(jnp.bfloat16)
    low = (table - high.astype(np.float32)).astype(jnp.bfloat16)
    v = np.arange(16)[:, None] + 16 * np.arange(8)[None, :]
    angle = 2.0 * np.pi / FREQS * (v[:, :, None] * np.arange(256)[None, None, :])
    last = (np.stack([np.cos(angle), np.sin(angle)]) / FREQS).astype(np.float32)
    angle = 2.0 * np.pi / 128 * (np.arange(8)[:, None] * np.arange(16)[None, :])
    first = np.stack([np.cos(angle), np.sin(angle)], axis=-1).astype(np.float32)
    return high, low, last, first.reshape(-1)


def kernel(
    u_hbm, g_hbm, decay_ref, w_first_ref, w_second_ref, w_out_ref, m_first_ref, m_second_ref, m_out_ref,
    dft_high_ref, dft_low_ref, last_ref, first_ref,
    step_first_ref, step_second_ref, step_out_ref,
    u_buf, g_buf, in_sem,
    send1, recv1, ssem1, rsem1,
    mid, x_high, x_low, decay_rows, window,
    feats, wf, act_one, cos_one, act_two, cos_two,
    send2, recv2, ssem2, rsem2,
    go_send, go_recv, ssem3, rsem3,
    go_sum, go_all, ssem4, rsem4,
    pay, ar_send, ar_recv, ssem5, rsem5,
    ch_send, ch_recv, ssem6, rsem6,
    ag_send, ag_recv, ssem7, rsem7,
):
    me = lax.axis_index("dp")
    col = lax.axis_index("chan")

    def dp_peer(i):
        return lax.rem(me + i, DP)

    def ch_peer(i):
        return lax.rem(col + i, CHAN)

    def to_dp(src, dst, ssem, rsem, peer):
        return pltpu.make_async_remote_copy(
            src_ref=src, dst_ref=dst, send_sem=ssem, recv_sem=rsem, device_id=(peer, col), device_id_type=MESH
        )

    def to_ch(src, dst, ssem, rsem, peer):
        return pltpu.make_async_remote_copy(
            src_ref=src, dst_ref=dst, send_sem=ssem, recv_sem=rsem, device_id=(me, peer), device_id_type=MESH
        )

    def loop(low, high, body):
        def wrapped(i, carry):
            body(i)
            return carry

        lax.fori_loop(low, high, wrapped, 0)

    def in_copy(block, which):
        hbm, buf = ((u_hbm, u_buf), (g_hbm, g_buf))[which]
        lanes = pl.ds(block * 128, 128)
        return pltpu.make_async_copy(hbm.at[:, :, lanes], buf.at[:, :, lanes], in_sem.at[2 * block + which])

    for block in range(2):
        for which in range(2):
            in_copy(block, which).start()

    barrier = pltpu.get_barrier_semaphore()

    def greet_dp(i):
        pl.semaphore_signal(barrier, inc=1, device_id=(dp_peer(i), col), device_id_type=MESH)

    def greet_ch(i):
        pl.semaphore_signal(barrier, inc=1, device_id=(me, ch_peer(i)), device_id_type=MESH)

    loop(1, DP, greet_dp)
    loop(1, CHAN, greet_ch)

    for block in range(2):
        for which in range(2):
            in_copy(block, which).wait()

        def product(kt, block=block):
            rows = pl.ds(pl.multiple_of(kt * 128, 128), 128)
            lanes = pl.ds(block * 128, 128)
            u_re, u_im = u_buf[0, rows, lanes], u_buf[1, rows, lanes]
            g_re, g_im = g_buf[0, rows, lanes], g_buf[1, rows, lanes]
            re = g_re * u_re + g_im * u_im
            im = g_im * u_re - g_re * u_im
            owners = pl.ds(block * 16, 16)
            send1[owners, 0, :, rows] = re.T.reshape(16, 8, 128)
            send1[owners, 1, :, rows] = im.T.reshape(16, 8, 128)

        loop(0, ROWS // 128, product)
        if block == 0:
            pl.semaphore_wait(barrier, DP - 1 + CHAN - 1)

        def send(i, block=block):
            peer = block * 16 + lax.rem(me + i, 16)

            @pl.when(peer != me)
            def _():
                to_dp(send1.at[peer], recv1.at[me], ssem1.at[peer], rsem1.at[me], peer).start()

        loop(0, 16, send)
    recv1[me] = send1[me]

    decay_rows[...] = jnp.broadcast_to(decay_ref[...], (128, COLS)).T
    decay = decay_rows[pl.ds(pl.multiple_of(me * 8, 8), 8), :]
    lane = lax.broadcasted_iota(jnp.int32, (8, 128), 1)

    def make_window(v):
        t = lax.div(v, 8) + 16 * lax.rem(v, 8) + 128 * lane
        window[pl.ds(pl.multiple_of(v * 8, 8), 8), :] = jnp.exp(-t.astype(jnp.float32) / decay)

    loop(0, 128, make_window)

    column = lax.broadcasted_iota(jnp.int32, (16, 512), 1)
    position = lax.div(me, 2) + 16 * (4 * lax.rem(me, 2) + (column >> 7)) + 128 * (column & 127)
    band = lax.broadcasted_iota(jnp.int32, (16, 512), 0) + 1
    angle = 2.0 * math.pi / SEQ * ((band * position) & (SEQ - 1)).astype(jnp.float32)
    feats[...] = jnp.zeros_like(feats)
    feats[0:16, :] = jnp.cos(angle)
    feats[16:32, :] = jnp.sin(angle)
    feats[32:33, :] = position[0:1, :].astype(jnp.float32) / SEQ
    wf[...] = jnp.zeros_like(wf)
    wf[0:32, 0:HID] = w_first_ref[1:33, :]
    wf[32:33, 0:HID] = w_first_ref[0:1, :]
    pre_one = jnp.dot(wf[...].T[0:HID, :], feats[...], precision=HIGHEST, preferred_element_type=jnp.float32)
    act_one[...] = jnp.sin(pre_one)
    cos_one[...] = jnp.cos(pre_one)
    wf[0:HID, 0:HID] = w_second_ref[...]
    wf[HID:, :] = jnp.zeros((128 - HID, 128), jnp.float32)
    pre_two = jnp.dot(
        wf[...].T[0:HID, 0:HID], act_one[...], precision=HIGHEST, preferred_element_type=jnp.float32
    )
    act_two[...] = jnp.sin(pre_two)
    cos_two[...] = jnp.cos(pre_two)
    go_send[...] = jnp.zeros_like(go_send)
    pay[...] = jnp.zeros_like(pay)

    def arrived1(i):
        peer = dp_peer(i)
        to_dp(send1.at[peer], recv1.at[peer], ssem1.at[peer], rsem1.at[peer], peer).wait_recv()

    loop(1, DP, arrived1)

    def pass_one(n):
        q0, lt = lax.div(n, 2), lax.rem(n, 2)
        half, k1 = lax.div(q0, 4), lax.rem(q0, 4)
        lanes = pl.ds(pl.multiple_of(k1 * 256 + lt * 128, 128), 128)
        out_lanes = pl.ds(pl.multiple_of(lt * 128, 128), 128)
        values = dft([(recv1[2 * q + half, 0, :, lanes], recv1[2 * q + half, 1, :, lanes]) for q in range(16)])
        for v1 in range(16):
            re, im = values[v1]
            if v1 > 0:
                c, s = first_ref[q0 * 32 + 2 * v1], first_ref[q0 * 32 + 2 * v1 + 1]
                re, im = re * c - im * s, re * s + im * c
            mid[v1, q0, 0, :, out_lanes] = re
            mid[v1, q0, 1, :, out_lanes] = im

    loop(0, 16, pass_one)

    def pass_two(n):
        v1, lt = lax.div(n, 2), lax.rem(n, 2)
        lanes = pl.ds(pl.multiple_of(lt * 128, 128), 128)
        im_lanes = pl.ds(pl.multiple_of(256 + lt * 128, 128), 128)
        values = dft([(mid[v1, q0, 0, :, lanes], mid[v1, q0, 1, :, lanes]) for q0 in range(8)])
        turned = []
        for v2 in range(8):
            re, im = values[v2]
            c = last_ref[0, v1, v2 : v2 + 1, lanes]
            s = last_ref[1, v1, v2 : v2 + 1, lanes]
            turned.append((re * c - im * s, re * s + im * c))
        for pair in range(4):
            rows = pl.ds(pl.multiple_of(v1 * 64 + pair * 16, 16), 16)
            for part, where in ((0, lanes), (1, im_lanes)):
                x = jnp.concatenate([turned[2 * pair][part], turned[2 * pair + 1][part]], axis=0)
                high, low = split(x)
                x_high[rows, where] = high
                x_low[rows, where] = low

    loop(0, 32, pass_two)

    def out_block(n):
        rows = pl.ds(pl.multiple_of(n * 256, 256), 256)
        x = (x_high[rows, :], x_low[rows, :])
        y = dot3(x, (dft_high_ref[...], dft_low_ref[...]), NN) * window[rows, :]
        send2[pl.ds(n * 8, 8), :, :] = y.reshape(8, 32, 128)

        def send(i):
            peer = n * 8 + lax.rem(me + i, 8)

            @pl.when(peer != me)
            def _():
                to_dp(send2.at[peer], recv2.at[me], ssem2.at[peer], rsem2.at[me], peer).start()

        loop(0, 8, send)

    loop(0, 4, out_block)
    recv2[me] = send2[me]

    def arrived2(i):
        peer = dp_peer(i)
        to_dp(send2.at[peer], recv2.at[peer], ssem2.at[peer], rsem2.at[peer], peer).wait_recv()

    loop(1, DP, arrived2)

    out_grad = [split(recv2[:, 8 * j : 8 * j + 8, :].reshape(COLS, 128)) for j in range(4)]
    grad_out = jnp.zeros((COLS, HID), jnp.float32)
    for j in range(4):
        grad_out += dot3(out_grad[j], split(act_two[:, 128 * j : 128 * j + 128]), NT)
    go_send[:, :, 0:HID] = grad_out.reshape(DP, 8, HID)

    def send_go(i):
        peer = dp_peer(i)
        to_dp(go_send.at[peer], go_recv.at[me], ssem3.at[peer], rsem3.at[me], peer).start()

    loop(1, DP, send_go)
    go_recv[me] = go_send[me]

    w_out_parts = split(w_out_ref[...])
    w_second_parts = split(w_second_ref[...])
    grad_second = jnp.zeros((HID, HID), jnp.float32)
    grad_first = jnp.zeros((40, HID), jnp.float32)
    for j in range(4):
        cols = slice(128 * j, 128 * j + 128)
        hidden = dot3(w_out_parts, out_grad[j], NN)
        back_two = split(hidden * cos_two[:, cols])
        grad_second += dot3(split(act_one[:, cols]), back_two, NT)
        back_one = split(dot3(w_second_parts, back_two, NN) * cos_one[:, cols])
        grad_first += dot3(split(feats[0:40, cols]), back_one, NT)
    pay[0:32, :] = jnp.concatenate([grad_second[0:32], grad_second[32:64]], axis=1)
    pay[32:48, :] = jnp.concatenate([grad_first[0:16], grad_first[16:32]], axis=1)
    pay[48:49, 0:HID] = grad_first[32:33]

    def arrived_go(i):
        peer = dp_peer(i)
        to_dp(go_send.at[peer], go_recv.at[peer], ssem3.at[peer], rsem3.at[peer], peer).wait_recv()

    loop(1, DP, arrived_go)
    total_out = jnp.sum(go_recv[...], axis=0)
    go_sum[...] = total_out
    go_all[me] = total_out

    def send_go_all(i):
        peer = dp_peer(i)
        to_dp(go_sum, go_all.at[me], ssem4.at[peer], rsem4.at[me], peer).start()

    loop(1, DP, send_go_all)
    pay[49:50, :] = jnp.sum(total_out * total_out, axis=0, keepdims=True)

    for i in range(DP):
        ar_send[i] = pay[2 * i : 2 * i + 2, :]

    def send_ar(i):
        peer = dp_peer(i)
        to_dp(ar_send.at[peer], ar_recv.at[me], ssem5.at[peer], rsem5.at[me], peer).start()

    loop(1, DP, send_ar)
    ar_recv[me] = ar_send[me]

    def arrived_ar(i):
        peer = dp_peer(i)
        to_dp(ar_send.at[peer], ar_recv.at[peer], ssem5.at[peer], rsem5.at[peer], peer).wait_recv()

    loop(1, DP, arrived_ar)
    ch_send[...] = jnp.sum(ar_recv[...], axis=0)

    def send_ch(i):
        peer = ch_peer(i)
        to_ch(ch_send, ch_recv.at[col], ssem6.at[peer], rsem6.at[col], peer).start()

    loop(1, CHAN, send_ch)
    ch_recv[col] = ch_send[...]

    def arrived_ch(i):
        peer = ch_peer(i)
        to_ch(ch_send, ch_recv.at[peer], ssem6.at[peer], rsem6.at[peer], peer).wait_recv()

    loop(1, CHAN, arrived_ch)
    ag_send[...] = jnp.sum(ch_recv[...], axis=0)

    def send_ag(i):
        peer = dp_peer(i)
        to_dp(ag_send, ag_recv.at[me], ssem7.at[peer], rsem7.at[me], peer).start()

    loop(1, DP, send_ag)
    ag_recv[me] = ag_send[...]

    def arrived_go_all(i):
        peer = dp_peer(i)
        to_dp(go_sum, go_all.at[peer], ssem4.at[peer], rsem4.at[peer], peer).wait_recv()

    loop(1, DP, arrived_go_all)
    full_out = go_all[...].reshape(COLS, 128).T[0:HID, :]

    def arrived_ag(i):
        peer = dp_peer(i)
        to_dp(ag_send, ag_recv.at[peer], ssem7.at[peer], rsem7.at[peer], peer).wait_recv()

    loop(1, DP, arrived_ag)
    for i in range(DP):
        pay[2 * i : 2 * i + 2, :] = ag_recv[i]
    second = pay[0:32, :]
    first = pay[32:48, :]
    line = pay[48:49, 0:HID]
    total = (
        jnp.sum(second * second, keepdims=True)
        + jnp.sum(first * first, keepdims=True)
        + jnp.sum(line * line, keepdims=True)
        + jnp.sum(pay[49:50, :], keepdims=True)
    )
    scale = jnp.minimum(1.0, clip_norm / (jnp.sqrt(total) + 1e-06))
    step_out_ref[...] = adam_step(full_out, w_out_ref[...], m_out_ref[0], m_out_ref[1], scale)
    for part in range(2):
        rows, lanes = slice(32 * part, 32 * part + 32), slice(HID * part, HID * part + HID)
        step_second_ref[rows, :] = adam_step(
            second[:, lanes], w_second_ref[rows, :], m_second_ref[0, rows, :], m_second_ref[1, rows, :], scale
        )
        rows = slice(16 * part + 1, 16 * part + 17)
        step_first_ref[rows, :] = adam_step(
            first[:, lanes], w_first_ref[rows, :], m_first_ref[0, rows, :], m_first_ref[1, rows, :], scale
        )
    step_first_ref[0:1, :] = adam_step(
        line, w_first_ref[0:1, :], m_first_ref[0, 0:1, :], m_first_ref[1, 0:1, :], scale
    )

    def sent_dp(i):
        peer = dp_peer(i)
        to_dp(send1.at[peer], recv1.at[me], ssem1.at[peer], rsem1.at[me], peer).wait_send()
        to_dp(send2.at[peer], recv2.at[me], ssem2.at[peer], rsem2.at[me], peer).wait_send()
        to_dp(go_send.at[peer], go_recv.at[me], ssem3.at[peer], rsem3.at[me], peer).wait_send()
        to_dp(go_sum, go_all.at[me], ssem4.at[peer], rsem4.at[me], peer).wait_send()
        to_dp(ar_send.at[peer], ar_recv.at[me], ssem5.at[peer], rsem5.at[me], peer).wait_send()
        to_dp(ag_send, ag_recv.at[me], ssem7.at[peer], rsem7.at[me], peer).wait_send()

    loop(1, DP, sent_dp)

    def sent_ch(i):
        peer = ch_peer(i)
        to_ch(ch_send, ch_recv.at[col], ssem6.at[peer], rsem6.at[col], peer).wait_send()

    loop(1, CHAN, sent_ch)


def local(spec_u, spec_g, decay_length, w_first, w_second, w_out, moments_first, moments_second, moments_out):
    dft_high, dft_low, last, first = constants()
    f32, bf16 = jnp.float32, jnp.bfloat16
    vmem, sem = pltpu.VMEM, pltpu.SemaphoreType.DMA
    in_vmem = pl.BlockSpec(memory_space=pltpu.VMEM)
    anywhere = pl.BlockSpec(memory_space=pl.ANY)

    def pair(n):
        return [sem((n,)), sem((n,))]

    return pl.pallas_call(
        kernel,
        out_shape=(
            jax.ShapeDtypeStruct(w_first.shape, f32),
            jax.ShapeDtypeStruct(w_second.shape, f32),
            jax.ShapeDtypeStruct(w_out.shape, f32),
        ),
        in_specs=[anywhere] * 2 + [in_vmem] * 10 + [pl.BlockSpec(memory_space=pltpu.SMEM)],
        out_specs=(in_vmem,) * 3,
        scratch_shapes=[
            vmem((2, ROWS, COLS), f32), vmem((2, ROWS, COLS), f32), sem((4,)),
            vmem((DP, 2, 8, ROWS), f32), vmem((DP, 2, 8, ROWS), f32), *pair(DP),
            vmem((16, 8, 2, 8, 256), f32), vmem((1024, 512), bf16), vmem((1024, 512), bf16),
            vmem((COLS, 128), f32), vmem((1024, 128), f32),
            vmem((128, 512), f32), vmem((128, 128), f32),
            vmem((HID, 512), f32), vmem((HID, 512), f32), vmem((HID, 512), f32), vmem((HID, 512), f32),
            vmem((DP, 32, 128), f32), vmem((DP, 32, 128), f32), *pair(DP),
            vmem((DP, 8, 128), f32), vmem((DP, 8, 128), f32), *pair(DP),
            vmem((8, 128), f32), vmem((DP, 8, 128), f32), *pair(DP),
            vmem((64, 128), f32), vmem((DP, 2, 128), f32), vmem((DP, 2, 128), f32), *pair(DP),
            vmem((2, 128), f32), vmem((CHAN, 2, 128), f32), *pair(CHAN),
            vmem((2, 128), f32), vmem((DP, 2, 128), f32), *pair(DP),
        ],
        compiler_params=pltpu.CompilerParams(
            collective_id=0, has_side_effects=True, vmem_limit_bytes=40 * 1024 * 1024
        ),
        name="hyena_step",
    )(
        spec_u, spec_g, decay_length.reshape(1, COLS), w_first, w_second, w_out,
        moments_first, moments_second, moments_out,
        jnp.asarray(dft_high), jnp.asarray(dft_low), jnp.asarray(last), jnp.asarray(first),
    )


def solution(mesh):
    return jax.shard_map(
        local,
        mesh=mesh,
        in_specs=(
            P(None, "dp", "chan"),
            P(None, "dp", "chan"),
            P("chan"),
            P(),
            P(),
            P(None, "chan"),
            P(),
            P(),
            P(None, None, "chan"),
        ),
        out_specs=(P(), P(), P(None, "chan")),
        check_vma=False,
    )
```

time: 597 us -> 130 us (0.22)
  the two profiles are of different devices: /device:TPU:24 before, /device:TPU:1 now
where the time goes in v1:
time: 130 us
  Pallas kernels  115 us (88%)
  local copies, waits for them, and re-layouts  14 us (11%)
    pallas_call x1, Pallas kernels, local(): pl.pallas_call(kernel, out_shape=(jax.ShapeDtypeStruct(w_first.shape, f32...  115 us
    unnamed x28, local copies, waits for them, and re-layouts  14 us

profile of v1, /device:TPU:1, one launch (start us, length us, event | category | flops | bytes accessed | tf_op | source)
XLA Modules:
  0.0 129.8 jit_solution(3810773778019486689)
XLA Ops:
  0.6 0.8 copy.16.m_first_ref
  1.4 0.0 copy-start
  1.4 1.6 %copy-done = f32[2,1024,256]{2,1,0:T(8,128)S(1)} copy-done((f32[2,1024,256]{2,1,0:T(8,128)S(1)}, f32[2,1024,256]{2,1,0:T(8,128)}, u32[]{:S(2)}) %copy-start) | copy-done | bytes 2097176
  3.0 0.0 copy-start.1
  3.0 1.6 %copy-done.1 = f32[2,1024,256]{2,1,0:T(8,128)S(1)} copy-done((f32[2,1024,256]{2,1,0:T(8,128)S(1)}, f32[2,1024,256]{2,1,0:T(8,128)}, u32[]{:S(2)}) %copy-start.1) | copy-done | bytes 2097176
  4.6 0.0 copy-start.2
  4.6 0.9 copy-done.2
  5.5 0.0 copy-start.3
  5.5 0.9 copy-done.3
  6.4 0.0 copy-start.4
  6.4 0.9 copy-done.4
  7.3 0.0 copy-start.5
  7.3 0.9 copy-done.5
  8.2 0.0 copy-start.6
  8.2 0.8 copy-done.6
  9.1 0.0 copy-start.7
  9.1 0.8 copy-done.7
  9.9 0.0 copy-start.8
  9.9 0.8 copy-done.8
  10.7 0.0 copy-start.9
  10.7 0.7 copy-done.9
  11.4 0.0 copy-start.10
  11.4 0.7 copy-done.10
  12.1 0.0 copy-start.11
  12.1 0.7 copy-done.11
  12.8 115.2 %hyena_step.1 = (f32[33,64]{1,0:T(8,128)S(1)}, f32[64,64]{1,0:T(8,128)S(1)}, f32[64,256]{1,0:T(8,128)S(1)}) custom-call(f32[2,1024,256]{2,1,0:T(8,128)S(1)} %copy-done, f32[2,1024,256]{2,1,0:T(8,128)S(1)} %copy-done.1, f32[1,256]{1,0:T(1,128)S(1)} %bitcast.1, f32[33,64]{1,0:T(8,128)S(1)} %copy-done.9, f32[64,64]{1,0:T(8,128)S(1)} %copy-done.8, ...), custom_call_target="tpu_custom_call" | custom-call | tf_op jit(solution)/shard_map/hyena_step/pallas_call | solution.py:445
  128.0 0.6 copy.20
  128.6 0.6 copy.21
  129.2 0.6 copy.22
Async XLA Ops:
  1.4 1.6 %copy-start = (f32[2,1024,256]{2,1,0:T(8,128)S(1)}, f32[2,1024,256]{2,1,0:T(8,128)}, u32[]{:S(2)}) copy-start(f32[2,1024,256]{2,1,0:T(8,128)} %u_hbm.1) | copy-start | bytes 6291460
  3.0 1.6 %copy-start.1 = (f32[2,1024,256]{2,1,0:T(8,128)S(1)}, f32[2,1024,256]{2,1,0:T(8,128)}, u32[]{:S(2)}) copy-start(f32[2,1024,256]{2,1,0:T(8,128)} %g_hbm.1) | copy-start | bytes 6291460
  4.6 0.9 copy-start.2
  5.5 0.9 copy-start.3
  6.4 0.9 copy-start.4
  7.3 0.9 copy-start.5
  8.2 0.8 copy-start.6
  9.1 0.8 copy-start.7
  9.9 0.8 copy-start.8
  10.7 0.7 copy-start.9
  11.4 0.7 copy-start.10
  12.1 0.7 copy-start.11

commit v2 on v1

--- a/solution.py
+++ b/solution.py
@@ -104,10 +104,12 @@
 
 
 def kernel(
-    u_hbm, g_hbm, decay_ref, w_first_ref, w_second_ref, w_out_ref, m_first_ref, m_second_ref, m_out_ref,
-    dft_high_ref, dft_low_ref, last_ref, first_ref,
+    u_hbm, g_hbm, decay_hbm, w_first_hbm, w_second_hbm, w_out_hbm, m_first_hbm, m_second_hbm, m_out_hbm,
+    dft_high_hbm, dft_low_hbm, last_hbm, first_hbm,
     step_first_ref, step_second_ref, step_out_ref,
     u_buf, g_buf, in_sem,
+    decay_ref, w_first_ref, w_second_ref, w_out_ref, m_first_ref, m_second_ref, m_out_ref,
+    dft_high_ref, dft_low_ref, last_ref, first_ref, small_sem,
     send1, recv1, ssem1, rsem1,
     mid, x_high, x_low, decay_rows, window,
     feats, wf, act_one, cos_one, act_two, cos_two,
@@ -127,6 +129,14 @@
     def ch_peer(i):
         return lax.rem(col + i, CHAN)
 
+    def chunk_of(device):
+        return lax.rem(device, 2) * 16 + lax.div(device, 2)
+
+    def places_of(device):
+        return lax.rem(device, 4) * 8 + lax.div(device, 4)
+
+    mine = chunk_of(me)
+
     def to_dp(src, dst, ssem, rsem, peer):
         return pltpu.make_async_remote_copy(
             src_ref=src, dst_ref=dst, send_sem=ssem, recv_sem=rsem, device_id=(peer, col), device_id_type=MESH
@@ -144,6 +154,25 @@
 
         lax.fori_loop(low, high, wrapped, 0)
 
+    def sent(phases):
+        def sent_dp(i):
+            peer = dp_peer(i)
+            copies = [
+                (send1.at[peer], recv1, ssem1, rsem1), (send2.at[peer], recv2, ssem2, rsem2),
+                (go_send.at[peer], go_recv, ssem3, rsem3), (go_sum, go_all, ssem4, rsem4),
+                (ar_send.at[peer], ar_recv, ssem5, rsem5), (ag_send, ag_recv, ssem7, rsem7),
+            ]
+            for src, dst, ssem, rsem in copies[: min(phases, 6)]:
+                to_dp(src, dst.at[me], ssem.at[peer], rsem.at[me], peer).wait_send()
+
+        loop(1, DP, sent_dp)
+
+        def sent_ch(i):
+            peer = ch_peer(i)
+            to_ch(ch_send, ch_recv.at[col], ssem6.at[peer], rsem6.at[col], peer).wait_send()
+
+        loop(1, CHAN, sent_ch)
+
     def in_copy(block, which):
         hbm, buf = ((u_hbm, u_buf), (g_hbm, g_buf))[which]
         lanes = pl.ds(block * 128, 128)
@@ -152,6 +181,16 @@
     for block in range(2):
         for which in range(2):
             in_copy(block, which).start()
+
+    small = [
+        pltpu.make_async_copy(src, dst, small_sem.at[n])
+        for n, (src, dst) in enumerate((
+            (decay_hbm, decay_ref), (w_first_hbm, w_first_ref), (w_second_hbm, w_second_ref),
+            (w_out_hbm, w_out_ref), (m_first_hbm, m_first_ref), (m_second_hbm, m_second_ref),
+            (m_out_hbm, m_out_ref), (dft_high_hbm, dft_high_ref), (dft_low_hbm, dft_low_ref),
+            (last_hbm, last_ref), (first_hbm, first_ref),
+        ))
+    ]
 
     barrier = pltpu.get_barrier_semaphore()
 
@@ -184,17 +223,22 @@
             pl.semaphore_wait(barrier, DP - 1 + CHAN - 1)
 
         def send(i, block=block):
-            peer = block * 16 + lax.rem(me + i, 16)
+            n = lax.rem(lax.div(me, 2) + i, 16)
+            peer = 2 * n + block
 
             @pl.when(peer != me)
             def _():
-                to_dp(send1.at[peer], recv1.at[me], ssem1.at[peer], rsem1.at[me], peer).start()
+                to_dp(send1.at[block * 16 + n], recv1.at[me], ssem1.at[peer], rsem1.at[me], peer).start()
 
         loop(0, 16, send)
-    recv1[me] = send1[me]
+    for copy in small:
+        copy.start()
+    recv1[me] = send1[mine]
+    for copy in small:
+        copy.wait()
 
     decay_rows[...] = jnp.broadcast_to(decay_ref[...], (128, COLS)).T
-    decay = decay_rows[pl.ds(pl.multiple_of(me * 8, 8), 8), :]
+    decay = decay_rows[pl.ds(pl.multiple_of(mine * 8, 8), 8), :]
     lane = lax.broadcasted_iota(jnp.int32, (8, 128), 1)
 
     def make_window(v):
@@ -204,7 +248,8 @@
     loop(0, 128, make_window)
 
     column = lax.broadcasted_iota(jnp.int32, (16, 512), 1)
-    position = lax.div(me, 2) + 16 * (4 * lax.rem(me, 2) + (column >> 7)) + 128 * (column & 127)
+    place = places_of(me)
+    position = lax.div(place, 2) + 16 * (4 * lax.rem(place, 2) + (column >> 7)) + 128 * (column & 127)
     band = lax.broadcasted_iota(jnp.int32, (16, 512), 0) + 1
     angle = 2.0 * math.pi / SEQ * ((band * position) & (SEQ - 1)).astype(jnp.float32)
     feats[...] = jnp.zeros_like(feats)
@@ -226,6 +271,7 @@
     cos_two[...] = jnp.cos(pre_two)
     go_send[...] = jnp.zeros_like(go_send)
     pay[...] = jnp.zeros_like(pay)
+    ch_send[...] = jnp.zeros_like(ch_send)
 
     def arrived1(i):
         peer = dp_peer(i)
@@ -277,16 +323,17 @@
         send2[pl.ds(n * 8, 8), :, :] = y.reshape(8, 32, 128)
 
         def send(i):
-            peer = n * 8 + lax.rem(me + i, 8)
+            z = lax.rem(lax.div(me, 4) + i, 8)
+            peer = 4 * z + n
 
             @pl.when(peer != me)
             def _():
-                to_dp(send2.at[peer], recv2.at[me], ssem2.at[peer], rsem2.at[me], peer).start()
+                to_dp(send2.at[n * 8 + z], recv2.at[mine], ssem2.at[peer], rsem2.at[me], peer).start()
 
         loop(0, 8, send)
 
     loop(0, 4, out_block)
-    recv2[me] = send2[me]
+    recv2[mine] = send2[places_of(me)]
 
     def arrived2(i):
         peer = dp_peer(i)
@@ -302,10 +349,10 @@
 
     def send_go(i):
         peer = dp_peer(i)
-        to_dp(go_send.at[peer], go_recv.at[me], ssem3.at[peer], rsem3.at[me], peer).start()
+        to_dp(go_send.at[chunk_of(peer)], go_recv.at[me], ssem3.at[peer], rsem3.at[me], peer).start()
 
     loop(1, DP, send_go)
-    go_recv[me] = go_send[me]
+    go_recv[me] = go_send[mine]
 
     w_out_parts = split(w_out_ref[...])
     w_second_parts = split(w_second_ref[...])
@@ -322,6 +369,16 @@
     pay[32:48, :] = jnp.concatenate([grad_first[0:16], grad_first[16:32]], axis=1)
     pay[48:49, 0:HID] = grad_first[32:33]
 
+    for i in range(DP):
+        ar_send[i] = pay[2 * i : 2 * i + 2, :]
+
+    def send_ar(i):
+        peer = dp_peer(i)
+        to_dp(ar_send.at[peer], ar_recv.at[me], ssem5.at[peer], rsem5.at[me], peer).start()
+
+    loop(1, DP, send_ar)
+    ar_recv[me] = ar_send[me]
+
     def arrived_go(i):
         peer = dp_peer(i)
         to_dp(go_send.at[peer], go_recv.at[peer], ssem3.at[peer], rsem3.at[peer], peer).wait_recv()
@@ -329,31 +386,21 @@
     loop(1, DP, arrived_go)
     total_out = jnp.sum(go_recv[...], axis=0)
     go_sum[...] = total_out
-    go_all[me] = total_out
+    go_all[mine] = total_out
 
     def send_go_all(i):
         peer = dp_peer(i)
-        to_dp(go_sum, go_all.at[me], ssem4.at[peer], rsem4.at[me], peer).start()
+        to_dp(go_sum, go_all.at[mine], ssem4.at[peer], rsem4.at[me], peer).start()
 
     loop(1, DP, send_go_all)
-    pay[49:50, :] = jnp.sum(total_out * total_out, axis=0, keepdims=True)
-
-    for i in range(DP):
-        ar_send[i] = pay[2 * i : 2 * i + 2, :]
-
-    def send_ar(i):
-        peer = dp_peer(i)
-        to_dp(ar_send.at[peer], ar_recv.at[me], ssem5.at[peer], rsem5.at[me], peer).start()
-
-    loop(1, DP, send_ar)
-    ar_recv[me] = ar_send[me]
+    ch_send[2:3, :] = jnp.sum(total_out * total_out, axis=0, keepdims=True)
 
     def arrived_ar(i):
         peer = dp_peer(i)
         to_dp(ar_send.at[peer], ar_recv.at[peer], ssem5.at[peer], rsem5.at[peer], peer).wait_recv()
 
     loop(1, DP, arrived_ar)
-    ch_send[...] = jnp.sum(ar_recv[...], axis=0)
+    ch_send[0:2, :] = jnp.sum(ar_recv[...], axis=0)
 
     def send_ch(i):
         peer = ch_peer(i)
@@ -389,7 +436,7 @@
 
     loop(1, DP, arrived_ag)
     for i in range(DP):
-        pay[2 * i : 2 * i + 2, :] = ag_recv[i]
+        pay[2 * i : 2 * i + 2, :] = ag_recv[i, 0:2, :]
     second = pay[0:32, :]
     first = pay[32:48, :]
     line = pay[48:49, 0:HID]
@@ -397,7 +444,7 @@
         jnp.sum(second * second, keepdims=True)
         + jnp.sum(first * first, keepdims=True)
         + jnp.sum(line * line, keepdims=True)
-        + jnp.sum(pay[49:50, :], keepdims=True)
+        + jnp.sum(jnp.sum(ag_recv[:, 2:3, :], axis=0), keepdims=True)
     )
     scale = jnp.minimum(1.0, clip_norm / (jnp.sqrt(total) + 1e-06))
     step_out_ref[...] = adam_step(full_out, w_out_ref[...], m_out_ref[0], m_out_ref[1], scale)
@@ -408,28 +455,13 @@
         )
         rows = slice(16 * part + 1, 16 * part + 17)
         step_first_ref[rows, :] = adam_step(
-            first[:, lanes], w_first_ref[rows, :], m_first_ref[0, rows, :], m_first_ref[1, rows, :], scale
+            first[:, lanes], w_first_ref[rows, :], m_first_ref[rows, 0, :], m_first_ref[rows, 1, :], scale
         )
     step_first_ref[0:1, :] = adam_step(
-        line, w_first_ref[0:1, :], m_first_ref[0, 0:1, :], m_first_ref[1, 0:1, :], scale
+        line, w_first_ref[0:1, :], m_first_ref[0:1, 0, :], m_first_ref[0:1, 1, :], scale
     )
 
-    def sent_dp(i):
-        peer = dp_peer(i)
-        to_dp(send1.at[peer], recv1.at[me], ssem1.at[peer], rsem1.at[me], peer).wait_send()
-        to_dp(send2.at[peer], recv2.at[me], ssem2.at[peer], rsem2.at[me], peer).wait_send()
-        to_dp(go_send.at[peer], go_recv.at[me], ssem3.at[peer], rsem3.at[me], peer).wait_send()
-        to_dp(go_sum, go_all.at[me], ssem4.at[peer], rsem4.at[me], peer).wait_send()
-        to_dp(ar_send.at[peer], ar_recv.at[me], ssem5.at[peer], rsem5.at[me], peer).wait_send()
-        to_dp(ag_send, ag_recv.at[me], ssem7.at[peer], rsem7.at[me], peer).wait_send()
-
-    loop(1, DP, sent_dp)
-
-    def sent_ch(i):
-        peer = ch_peer(i)
-        to_ch(ch_send, ch_recv.at[col], ssem6.at[peer], rsem6.at[col], peer).wait_send()
-
-    loop(1, CHAN, sent_ch)
+    sent(7)
 
 
 def local(spec_u, spec_g, decay_length, w_first, w_second, w_out, moments_first, moments_second, moments_out):
@@ -449,10 +481,14 @@
             jax.ShapeDtypeStruct(w_second.shape, f32),
             jax.ShapeDtypeStruct(w_out.shape, f32),
         ),
-        in_specs=[anywhere] * 2 + [in_vmem] * 10 + [pl.BlockSpec(memory_space=pltpu.SMEM)],
+        in_specs=[anywhere] * 13,
         out_specs=(in_vmem,) * 3,
         scratch_shapes=[
             vmem((2, ROWS, COLS), f32), vmem((2, ROWS, COLS), f32), sem((4,)),
+            vmem((1, COLS), f32), vmem((33, HID), f32), vmem((HID, HID), f32), vmem((HID, COLS), f32),
+            vmem((33, 2, HID), f32), vmem((2, HID, HID), f32), vmem((2, HID, COLS), f32),
+            vmem((512, 128), bf16), vmem((512, 128), bf16), vmem((2, 16, 8, 256), f32),
+            pltpu.SMEM((256,), f32), sem((11,)),
             vmem((DP, 2, 8, ROWS), f32), vmem((DP, 2, 8, ROWS), f32), *pair(DP),
             vmem((16, 8, 2, 8, 256), f32), vmem((1024, 512), bf16), vmem((1024, 512), bf16),
             vmem((COLS, 128), f32), vmem((1024, 128), f32),
@@ -462,16 +498,16 @@
             vmem((DP, 8, 128), f32), vmem((DP, 8, 128), f32), *pair(DP),
             vmem((8, 128), f32), vmem((DP, 8, 128), f32), *pair(DP),
             vmem((64, 128), f32), vmem((DP, 2, 128), f32), vmem((DP, 2, 128), f32), *pair(DP),
-            vmem((2, 128), f32), vmem((CHAN, 2, 128), f32), *pair(CHAN),
-            vmem((2, 128), f32), vmem((DP, 2, 128), f32), *pair(DP),
+            vmem((4, 128), f32), vmem((CHAN, 4, 128), f32), *pair(CHAN),
+            vmem((4, 128), f32), vmem((DP, 4, 128), f32), *pair(DP),
         ],
         compiler_params=pltpu.CompilerParams(
-            collective_id=0, has_side_effects=True, vmem_limit_bytes=40 * 1024 * 1024
+            collective_id=0, has_side_effects=True, vmem_limit_bytes=56 * 1024 * 1024
         ),
         name="hyena_step",
     )(
         spec_u, spec_g, decay_length.reshape(1, COLS), w_first, w_second, w_out,
-        moments_first, moments_second, moments_out,
+        jnp.swapaxes(moments_first, 0, 1), moments_second, moments_out,
         jnp.asarray(dft_high), jnp.asarray(dft_low), jnp.asarray(last), jnp.asarray(first),
     )
 

time: 130 us -> 115 us (0.88)
  local copies, waits for them, and re-layouts: 14 us -> 4.18 us
  Pallas kernels: 115 us -> 110 us
    unnamed x28 -> x3, local copies, waits for them, and re-layouts: 14 us -> 4.18 us
    pallas_call x1, Pallas kernels: 115 us -> 110 us  [local(): pl.pallas_call(kernel, out_shape=(jax.ShapeDtypeStruct(w_first.shape, f32...]
where the time goes in v2:
time: 115 us
  Pallas kernels  110 us (96%)
  local copies, waits for them, and re-layouts  4.18 us (4%)
    pallas_call x1, Pallas kernels, local(): pl.pallas_call(kernel, out_shape=(jax.ShapeDtypeStruct(w_first.shape, f32...  110 us
    unnamed x3, local copies, waits for them, and re-layouts  4.18 us

profile of v2, /device:TPU:1, one launch (start us, length us, event | category | flops | bytes accessed | tf_op | source)
XLA Modules:
  0.0 114.7 jit_solution(3606318359760028420)
XLA Ops:
  0.6 109.9 %hyena_step.1 = (f32[33,64]{1,0:T(8,128)}, f32[64,64]{1,0:T(8,128)}, f32[64,256]{1,0:T(8,128)}) custom-call(f32[2,1024,256]{2,1,0:T(8,128)} %u_hbm.1, f32[2,1024,256]{2,1,0:T(8,128)} %g_hbm.1, f32[1,256]{1,0:T(1,128)} %bitcast.3, f32[33,64]{1,0:T(8,128)} %w_first_hbm.1, f32[64,64]{1,0:T(8,128)} %w_second_hbm.1, f32[64,256]{1,0:T(8,128)} %w_out_hbm.1, ...), custom_call_target="tpu_custom_call" | custom-call | tf_op jit(solution)/shard_map/hyena_step/pallas_call | solution.py:477
  110.5 1.3 %copy.19 = f32[33,64]{1,0:T(8,128)} copy(f32[33,64]{1,0:T(8,128)} %get-tuple-element.6) | data formatting | bytes 16896
  111.9 1.4 %copy.20 = f32[64,64]{1,0:T(8,128)} copy(f32[64,64]{1,0:T(8,128)} %get-tuple-element.7) | data formatting | bytes 32768
  113.2 1.5 %copy.21 = f32[64,256]{1,0:T(8,128)} copy(f32[64,256]{1,0:T(8,128)} %get-tuple-element.8) | data formatting | bytes 131072

commit v3 on v2

--- a/solution.py
+++ b/solution.py
@@ -44,11 +44,39 @@
     return high, low
 
 
-def dot3(a, b, dims):
-    def one(x, y):
-        return lax.dot_general(x, y, (dims, ((), ())), preferred_element_type=jnp.float32)
-
-    return one(a[0], b[0]) + one(a[0], b[1]) + one(a[1], b[0])
+def dot(a, b, dims):
+    return lax.dot_general(a, b, (dims, ((), ())), preferred_element_type=jnp.float32)
+
+
+def stacked(x):
+    return jnp.concatenate(split(x), axis=0)
+
+
+def folded(x, rows):
+    x = x[:rows] + x[rows:]
+    return x[:, :HID] + x[:, HID:]
+
+
+def three_rows(x):
+    high, low = split(x)
+    return jnp.concatenate([high, low, high], axis=0)
+
+
+def three_lanes(x):
+    high, low = split(x)
+    return jnp.concatenate([high, high, low], axis=1)
+
+
+def sine_cosine(x):
+    turns = jnp.floor(x * (2.0 / math.pi) + 0.5)
+    r = ((x - turns * 1.5703125) - turns * 4.837512969970703125e-4) - turns * 7.54978995489188216e-8
+    z = r * r
+    sine = r + r * z * (-1.6666654611e-1 + z * (8.3321608736e-3 - z * 1.9515295891e-4))
+    cosine = 1.0 - 0.5 * z + z * z * (4.166664568298827e-2 + z * (-1.388731625493765e-3 + z * 2.443315711809948e-5))
+    quarter = turns.astype(jnp.int32)
+    odd = (quarter & 1) == 1
+    first, second = jnp.where(odd, cosine, sine), jnp.where(odd, sine, cosine)
+    return jnp.where((quarter & 2) == 2, -first, first), jnp.where(((quarter + 1) & 2) == 2, -second, second)
 
 
 NN = ((1,), (0,))
@@ -112,7 +140,7 @@
     dft_high_ref, dft_low_ref, last_ref, first_ref, small_sem,
     send1, recv1, ssem1, rsem1,
     mid, x_high, x_low, decay_rows, window,
-    feats, wf, act_one, cos_one, act_two, cos_two,
+    wf, w_rows, w_out_parts, w_second_parts, feats, act_one, cos_one, act_two, cos_two,
     send2, recv2, ssem2, rsem2,
     go_send, go_recv, ssem3, rsem3,
     go_sum, go_all, ssem4, rsem4,
@@ -132,10 +160,8 @@
     def chunk_of(device):
         return lax.rem(device, 2) * 16 + lax.div(device, 2)
 
-    def places_of(device):
-        return lax.rem(device, 4) * 8 + lax.div(device, 4)
-
     mine = chunk_of(me)
+    z, x = lax.div(me, 4), lax.rem(me, 4)
 
     def to_dp(src, dst, ssem, rsem, peer):
         return pltpu.make_async_remote_copy(
@@ -154,18 +180,24 @@
 
         lax.fori_loop(low, high, wrapped, 0)
 
-    def sent(phases):
+    def sent():
         def sent_dp(i):
             peer = dp_peer(i)
             copies = [
-                (send1.at[peer], recv1, ssem1, rsem1), (send2.at[peer], recv2, ssem2, rsem2),
-                (go_send.at[peer], go_recv, ssem3, rsem3), (go_sum, go_all, ssem4, rsem4),
+                (send1.at[peer], recv1, ssem1, rsem1), (go_sum, go_all, ssem4, rsem4),
                 (ar_send.at[peer], ar_recv, ssem5, rsem5), (ag_send, ag_recv, ssem7, rsem7),
             ]
-            for src, dst, ssem, rsem in copies[: min(phases, 6)]:
+            for src, dst, ssem, rsem in copies:
                 to_dp(src, dst.at[me], ssem.at[peer], rsem.at[me], peer).wait_send()
 
         loop(1, DP, sent_dp)
+
+        def sent_x(i):
+            n = lax.rem(x + i, 4)
+            to_dp(send2.at[n], recv2.at[x], ssem2.at[n], rsem2.at[x], 4 * z + n).wait_send()
+            to_dp(go_send.at[n], go_recv.at[x], ssem3.at[n], rsem3.at[x], 4 * z + n).wait_send()
+
+        loop(1, 4, sent_x)
 
         def sent_ch(i):
             peer = ch_peer(i)
@@ -247,28 +279,41 @@
 
     loop(0, 128, make_window)
 
-    column = lax.broadcasted_iota(jnp.int32, (16, 512), 1)
-    place = places_of(me)
-    position = lax.div(place, 2) + 16 * (4 * lax.rem(place, 2) + (column >> 7)) + 128 * (column & 127)
-    band = lax.broadcasted_iota(jnp.int32, (16, 512), 0) + 1
-    angle = 2.0 * math.pi / SEQ * ((band * position) & (SEQ - 1)).astype(jnp.float32)
-    feats[...] = jnp.zeros_like(feats)
-    feats[0:16, :] = jnp.cos(angle)
-    feats[16:32, :] = jnp.sin(angle)
-    feats[32:33, :] = position[0:1, :].astype(jnp.float32) / SEQ
+    w_rows[:, 0:HID] = w_out_ref[...].T
+    w_rows[:, HID:] = jnp.zeros((COLS, 128 - HID), jnp.float32)
+    met = [w_rows[pl.ds(pl.multiple_of(chunk_of(4 * z + n) * 8, 8), 8), :] for n in range(4)]
+    met = jnp.concatenate(met + [jnp.zeros((96, 128), jnp.float32)], axis=0).T
+    w_out_parts[...] = three_lanes(met[0:HID, 0:32])
+    w_second_parts[...] = three_lanes(w_second_ref[...])
+
     wf[...] = jnp.zeros_like(wf)
     wf[0:32, 0:HID] = w_first_ref[1:33, :]
     wf[32:33, 0:HID] = w_first_ref[0:1, :]
-    pre_one = jnp.dot(wf[...].T[0:HID, :], feats[...], precision=HIGHEST, preferred_element_type=jnp.float32)
-    act_one[...] = jnp.sin(pre_one)
-    cos_one[...] = jnp.cos(pre_one)
-    wf[0:HID, 0:HID] = w_second_ref[...]
-    wf[HID:, :] = jnp.zeros((128 - HID, 128), jnp.float32)
-    pre_two = jnp.dot(
-        wf[...].T[0:HID, 0:HID], act_one[...], precision=HIGHEST, preferred_element_type=jnp.float32
-    )
-    act_two[...] = jnp.sin(pre_two)
-    cos_two[...] = jnp.cos(pre_two)
+    wf[HID:, 0:HID] = w_second_ref[...]
+    turned = wf[...].T
+    w_first_t, w_second_t = turned[0:HID, 0:48], turned[0:HID, HID:]
+
+    def activations(n):
+        cols = pl.ds(pl.multiple_of(n * 512, 512), 512)
+        column = n * 512 + lax.broadcasted_iota(jnp.int32, (16, 512), 1)
+        residue = column >> 7
+        position = 4 * x + (residue >> 3) + 16 * (residue & 7) + 128 * (column & 127)
+        band = lax.broadcasted_iota(jnp.int32, (16, 512), 0) + 1
+        angle = 2.0 * math.pi / SEQ * ((band * position) & (SEQ - 1)).astype(jnp.float32)
+        sine, cosine = sine_cosine(angle)
+        ramp = jnp.where(band == 1, position.astype(jnp.float32) / SEQ, 0.0)
+        values = jnp.concatenate([cosine, sine, ramp], axis=0)
+        feats[:, cols] = stacked(values)
+        pre_one = jnp.dot(w_first_t, values, precision=HIGHEST, preferred_element_type=jnp.float32)
+        sine, cosine = sine_cosine(pre_one)
+        act_one[:, cols] = stacked(sine)
+        cos_one[:, cols] = cosine
+        pre_two = jnp.dot(w_second_t, sine, precision=HIGHEST, preferred_element_type=jnp.float32)
+        sine, cosine = sine_cosine(pre_two)
+        act_two[:, cols] = stacked(sine)
+        cos_two[:, cols] = cosine
+
+    loop(0, 8, activations)
     go_send[...] = jnp.zeros_like(go_send)
     pay[...] = jnp.zeros_like(pay)
     ch_send[...] = jnp.zeros_like(ch_send)
@@ -316,55 +361,43 @@
 
     loop(0, 32, pass_two)
 
-    def out_block(n):
+    def out_block(i):
+        n = lax.rem(x + 1 + i, 4)
         rows = pl.ds(pl.multiple_of(n * 256, 256), 256)
-        x = (x_high[rows, :], x_low[rows, :])
-        y = dot3(x, (dft_high_ref[...], dft_low_ref[...]), NN) * window[rows, :]
-        send2[pl.ds(n * 8, 8), :, :] = y.reshape(8, 32, 128)
-
-        def send(i):
-            z = lax.rem(lax.div(me, 4) + i, 8)
-            peer = 4 * z + n
-
-            @pl.when(peer != me)
-            def _():
-                to_dp(send2.at[n * 8 + z], recv2.at[mine], ssem2.at[peer], rsem2.at[me], peer).start()
-
-        loop(0, 8, send)
+        high, low = x_high[rows, :], x_low[rows, :]
+        y = dot(high, dft_high_ref[...], NN) + dot(high, dft_low_ref[...], NN) + dot(low, dft_high_ref[...], NN)
+        y = y * window[rows, :]
+        for v in range(32):
+            send2[n, :, 128 * v : 128 * v + 128] = y[8 * v : 8 * v + 8, :]
+
+        @pl.when(i < 3)
+        def _():
+            to_dp(send2.at[n], recv2.at[x], ssem2.at[n], rsem2.at[x], 4 * z + n).start()
 
     loop(0, 4, out_block)
-    recv2[mine] = send2[places_of(me)]
+    recv2[x] = send2[x]
+
+    def x_peer(i):
+        return lax.rem(x + i, 4)
 
     def arrived2(i):
-        peer = dp_peer(i)
-        to_dp(send2.at[peer], recv2.at[peer], ssem2.at[peer], rsem2.at[peer], peer).wait_recv()
-
-    loop(1, DP, arrived2)
-
-    out_grad = [split(recv2[:, 8 * j : 8 * j + 8, :].reshape(COLS, 128)) for j in range(4)]
-    grad_out = jnp.zeros((COLS, HID), jnp.float32)
+        n = x_peer(i)
+        to_dp(send2.at[n], recv2.at[n], ssem2.at[n], rsem2.at[n], 4 * z + n).wait_recv()
+
+    loop(1, 4, arrived2)
+
+    out_grad = recv2[...].reshape(32, 4096)
+    grad_second = jnp.zeros((2 * HID, 2 * HID), jnp.float32)
+    grad_first = jnp.zeros((96, 2 * HID), jnp.float32)
     for j in range(4):
-        grad_out += dot3(out_grad[j], split(act_two[:, 128 * j : 128 * j + 128]), NT)
-    go_send[:, :, 0:HID] = grad_out.reshape(DP, 8, HID)
-
-    def send_go(i):
-        peer = dp_peer(i)
-        to_dp(go_send.at[chunk_of(peer)], go_recv.at[me], ssem3.at[peer], rsem3.at[me], peer).start()
-
-    loop(1, DP, send_go)
-    go_recv[me] = go_send[mine]
-
-    w_out_parts = split(w_out_ref[...])
-    w_second_parts = split(w_second_ref[...])
-    grad_second = jnp.zeros((HID, HID), jnp.float32)
-    grad_first = jnp.zeros((40, HID), jnp.float32)
-    for j in range(4):
-        cols = slice(128 * j, 128 * j + 128)
-        hidden = dot3(w_out_parts, out_grad[j], NN)
-        back_two = split(hidden * cos_two[:, cols])
-        grad_second += dot3(split(act_one[:, cols]), back_two, NT)
-        back_one = split(dot3(w_second_parts, back_two, NN) * cos_one[:, cols])
-        grad_first += dot3(split(feats[0:40, cols]), back_one, NT)
+        cols = slice(1024 * j, 1024 * j + 1024)
+        hidden = dot(w_out_parts[...], three_rows(out_grad[:, cols]), NN)
+        high, low = split(hidden * cos_two[:, cols])
+        grad_second += dot(act_one[:, cols], jnp.concatenate([high, low], axis=0), NT)
+        back_one = dot(w_second_parts[...], jnp.concatenate([high, low, high], axis=0), NN) * cos_one[:, cols]
+        grad_first += dot(feats[:, cols], stacked(back_one), NT)
+    grad_second = folded(grad_second, HID)
+    grad_first = folded(grad_first, 48)
     pay[0:32, :] = jnp.concatenate([grad_second[0:32], grad_second[32:64]], axis=1)
     pay[32:48, :] = jnp.concatenate([grad_first[0:16], grad_first[16:32]], axis=1)
     pay[48:49, 0:HID] = grad_first[32:33]
@@ -379,11 +412,24 @@
     loop(1, DP, send_ar)
     ar_recv[me] = ar_send[me]
 
+    grad_out = jnp.zeros((2 * 32, 2 * HID), jnp.float32)
+    for j in range(4):
+        cols = slice(1024 * j, 1024 * j + 1024)
+        grad_out += dot(stacked(out_grad[:, cols]), act_two[:, cols], NT)
+    go_send[:, :, 0:HID] = folded(grad_out, 32).reshape(4, 8, HID)
+
+    def send_go(i):
+        n = x_peer(i)
+        to_dp(go_send.at[n], go_recv.at[x], ssem3.at[n], rsem3.at[x], 4 * z + n).start()
+
+    loop(1, 4, send_go)
+    go_recv[x] = go_send[x]
+
     def arrived_go(i):
-        peer = dp_peer(i)
-        to_dp(go_send.at[peer], go_recv.at[peer], ssem3.at[peer], rsem3.at[peer], peer).wait_recv()
-
-    loop(1, DP, arrived_go)
+        n = x_peer(i)
+        to_dp(go_send.at[n], go_recv.at[n], ssem3.at[n], rsem3.at[n], 4 * z + n).wait_recv()
+
+    loop(1, 4, arrived_go)
     total_out = jnp.sum(go_recv[...], axis=0)
     go_sum[...] = total_out
     go_all[mine] = total_out
@@ -461,7 +507,7 @@
         line, w_first_ref[0:1, :], m_first_ref[0:1, 0, :], m_first_ref[0:1, 1, :], scale
     )
 
-    sent(7)
+    sent()
 
 
 def local(spec_u, spec_g, decay_length, w_first, w_second, w_out, moments_first, moments_second, moments_out):
@@ -492,10 +538,11 @@
             vmem((DP, 2, 8, ROWS), f32), vmem((DP, 2, 8, ROWS), f32), *pair(DP),
             vmem((16, 8, 2, 8, 256), f32), vmem((1024, 512), bf16), vmem((1024, 512), bf16),
             vmem((COLS, 128), f32), vmem((1024, 128), f32),
-            vmem((128, 512), f32), vmem((128, 128), f32),
-            vmem((HID, 512), f32), vmem((HID, 512), f32), vmem((HID, 512), f32), vmem((HID, 512), f32),
-            vmem((DP, 32, 128), f32), vmem((DP, 32, 128), f32), *pair(DP),
-            vmem((DP, 8, 128), f32), vmem((DP, 8, 128), f32), *pair(DP),
+            vmem((128, 128), f32), vmem((COLS, 128), f32), vmem((HID, 96), bf16), vmem((HID, 192), bf16),
+            vmem((96, 4096), bf16), vmem((128, 4096), bf16), vmem((HID, 4096), f32),
+            vmem((128, 4096), bf16), vmem((HID, 4096), f32),
+            vmem((4, 8, 4096), f32), vmem((4, 8, 4096), f32), *pair(4),
+            vmem((4, 8, 128), f32), vmem((4, 8, 128), f32), *pair(4),
             vmem((8, 128), f32), vmem((DP, 8, 128), f32), *pair(DP),
             vmem((64, 128), f32), vmem((DP, 2, 128), f32), vmem((DP, 2, 128), f32), *pair(DP),
             vmem((4, 128), f32), vmem((CHAN, 4, 128), f32), *pair(CHAN),

time: 115 us -> 105 us (0.913)
  Pallas kernels: 110 us -> 99.9 us
    pallas_call x1, Pallas kernels: 110 us -> 99.9 us  [local(): pl.pallas_call(kernel, out_shape=(jax.ShapeDtypeStruct(w_first.shape, f32...]
where the time goes in v3:
time: 105 us
  Pallas kernels  99.9 us (95%)
  local copies, waits for them, and re-layouts  4.18 us (4%)
    pallas_call x1, Pallas kernels, local(): pl.pallas_call(kernel, out_shape=(jax.ShapeDtypeStruct(w_first.shape, f32...  99.9 us
    unnamed x3, local copies, waits for them, and re-layouts  4.18 us

profile of v3, /device:TPU:1, one launch (start us, length us, event | category | flops | bytes accessed | tf_op | source)
XLA Modules:
  0.0 104.7 jit_solution(1296937892905680224)
XLA Ops:
  0.6 99.9 %hyena_step.1 = (f32[33,64]{1,0:T(8,128)}, f32[64,64]{1,0:T(8,128)}, f32[64,256]{1,0:T(8,128)}) custom-call(f32[2,1024,256]{2,1,0:T(8,128)} %u_hbm.1, f32[2,1024,256]{2,1,0:T(8,128)} %g_hbm.1, f32[1,256]{1,0:T(1,128)} %bitcast.3, f32[33,64]{1,0:T(8,128)} %w_first_hbm.1, f32[64,64]{1,0:T(8,128)} %w_second_hbm.1, f32[64,256]{1,0:T(8,128)} %w_out_hbm.1, ...), custom_call_target="tpu_custom_call" | custom-call | tf_op jit(solution)/shard_map/hyena_step/pallas_call | solution.py:523
  100.5 1.3 %copy.19 = f32[33,64]{1,0:T(8,128)} copy(f32[33,64]{1,0:T(8,128)} %get-tuple-element.6) | data formatting | bytes 16896
  101.9 1.4 %copy.20 = f32[64,64]{1,0:T(8,128)} copy(f32[64,64]{1,0:T(8,128)} %get-tuple-element.7) | data formatting | bytes 32768
  103.3 1.5 %copy.21 = f32[64,256]{1,0:T(8,128)} copy(f32[64,256]{1,0:T(8,128)} %get-tuple-element.8) | data formatting | bytes 131072

commit v4 on v3

--- a/solution.py
+++ b/solution.py
@@ -173,37 +173,16 @@
             src_ref=src, dst_ref=dst, send_sem=ssem, recv_sem=rsem, device_id=(me, peer), device_id_type=MESH
         )
 
-    def loop(low, high, body):
+    def loop(low, high, body, unroll=False):
         def wrapped(i, carry):
             body(i)
             return carry
 
-        lax.fori_loop(low, high, wrapped, 0)
-
-    def sent():
-        def sent_dp(i):
-            peer = dp_peer(i)
-            copies = [
-                (send1.at[peer], recv1, ssem1, rsem1), (go_sum, go_all, ssem4, rsem4),
-                (ar_send.at[peer], ar_recv, ssem5, rsem5), (ag_send, ag_recv, ssem7, rsem7),
-            ]
-            for src, dst, ssem, rsem in copies:
-                to_dp(src, dst.at[me], ssem.at[peer], rsem.at[me], peer).wait_send()
-
-        loop(1, DP, sent_dp)
-
-        def sent_x(i):
-            n = lax.rem(x + i, 4)
-            to_dp(send2.at[n], recv2.at[x], ssem2.at[n], rsem2.at[x], 4 * z + n).wait_send()
-            to_dp(go_send.at[n], go_recv.at[x], ssem3.at[n], rsem3.at[x], 4 * z + n).wait_send()
-
-        loop(1, 4, sent_x)
-
-        def sent_ch(i):
-            peer = ch_peer(i)
-            to_ch(ch_send, ch_recv.at[col], ssem6.at[peer], rsem6.at[col], peer).wait_send()
-
-        loop(1, CHAN, sent_ch)
+        lax.fori_loop(low, high, wrapped, 0, unroll=unroll)
+
+    def sent_dp(i, src, dst, ssem, rsem):
+        peer = dp_peer(i)
+        to_dp(src, dst.at[me], ssem.at[peer], rsem.at[me], peer).wait_send()
 
     def in_copy(block, which):
         hbm, buf = ((u_hbm, u_buf), (g_hbm, g_buf))[which]
@@ -274,7 +253,7 @@
     lane = lax.broadcasted_iota(jnp.int32, (8, 128), 1)
 
     def make_window(v):
-        t = lax.div(v, 8) + 16 * lax.rem(v, 8) + 128 * lane
+        t = 4 * lax.rem(lax.div(v, 8), 4) + lax.div(v, 32) + 16 * lax.rem(v, 8) + 128 * lane
         window[pl.ds(pl.multiple_of(v * 8, 8), 8), :] = jnp.exp(-t.astype(jnp.float32) / decay)
 
     loop(0, 128, make_window)
@@ -352,7 +331,7 @@
             s = last_ref[1, v1, v2 : v2 + 1, lanes]
             turned.append((re * c - im * s, re * s + im * c))
         for pair in range(4):
-            rows = pl.ds(pl.multiple_of(v1 * 64 + pair * 16, 16), 16)
+            rows = pl.ds(pl.multiple_of(lax.rem(v1, 4) * 256 + lax.div(v1, 4) * 64 + pair * 16, 16), 16)
             for part, where in ((0, lanes), (1, im_lanes)):
                 x = jnp.concatenate([turned[2 * pair][part], turned[2 * pair + 1][part]], axis=0)
                 high, low = split(x)
@@ -361,40 +340,41 @@
 
     loop(0, 32, pass_two)
 
-    def out_block(i):
-        n = lax.rem(x + 1 + i, 4)
-        rows = pl.ds(pl.multiple_of(n * 256, 256), 256)
+    def x_peer(i):
+        return lax.rem(x + i, 4)
+
+    def to_x(i, j):
+        n, cols = x_peer(i), slice(1024 * j, 1024 * j + 1024)
+        return to_dp(send2.at[n, :, cols], recv2.at[x, :, cols], ssem2.at[n, j], rsem2.at[x, j], 4 * z + n)
+
+    def from_x(i, j):
+        n, cols = x_peer(i), slice(1024 * j, 1024 * j + 1024)
+        return to_dp(send2.at[n, :, cols], recv2.at[n, :, cols], ssem2.at[n, j], rsem2.at[n, j], 4 * z + n)
+
+    for j in range(4):
+        rows, cols = slice(256 * j, 256 * j + 256), slice(1024 * j, 1024 * j + 1024)
         high, low = x_high[rows, :], x_low[rows, :]
         y = dot(high, dft_high_ref[...], NN) + dot(high, dft_low_ref[...], NN) + dot(low, dft_high_ref[...], NN)
         y = y * window[rows, :]
-        for v in range(32):
-            send2[n, :, 128 * v : 128 * v + 128] = y[8 * v : 8 * v + 8, :]
-
-        @pl.when(i < 3)
-        def _():
-            to_dp(send2.at[n], recv2.at[x], ssem2.at[n], rsem2.at[x], 4 * z + n).start()
-
-    loop(0, 4, out_block)
-    recv2[x] = send2[x]
-
-    def x_peer(i):
-        return lax.rem(x + i, 4)
-
-    def arrived2(i):
-        n = x_peer(i)
-        to_dp(send2.at[n], recv2.at[n], ssem2.at[n], rsem2.at[n], 4 * z + n).wait_recv()
-
-    loop(1, 4, arrived2)
-
-    out_grad = recv2[...].reshape(32, 4096)
+        for n in range(4):
+            for v in range(8):
+                row, lanes = 64 * n + 8 * v, 1024 * j + 128 * v
+                send2[n, :, lanes : lanes + 128] = y[row : row + 8, :]
+        for i in (2, 1, 3):
+            to_x(i, j).start()
+        recv2[x, :, cols] = send2[x, :, cols]
+
+    w_parts, second_parts = w_out_parts[...], w_second_parts[...]
     grad_second = jnp.zeros((2 * HID, 2 * HID), jnp.float32)
     grad_first = jnp.zeros((96, 2 * HID), jnp.float32)
     for j in range(4):
         cols = slice(1024 * j, 1024 * j + 1024)
-        hidden = dot(w_out_parts[...], three_rows(out_grad[:, cols]), NN)
+        for i in (1, 3, 2):
+            from_x(i, j).wait_recv()
+        hidden = dot(w_parts, three_rows(recv2[:, :, cols].reshape(32, 1024)), NN)
         high, low = split(hidden * cos_two[:, cols])
         grad_second += dot(act_one[:, cols], jnp.concatenate([high, low], axis=0), NT)
-        back_one = dot(w_second_parts[...], jnp.concatenate([high, low, high], axis=0), NN) * cos_one[:, cols]
+        back_one = dot(second_parts, jnp.concatenate([high, low, high], axis=0), NN) * cos_one[:, cols]
         grad_first += dot(feats[:, cols], stacked(back_one), NT)
     grad_second = folded(grad_second, HID)
     grad_first = folded(grad_first, 48)
@@ -409,13 +389,13 @@
         peer = dp_peer(i)
         to_dp(ar_send.at[peer], ar_recv.at[me], ssem5.at[peer], rsem5.at[me], peer).start()
 
-    loop(1, DP, send_ar)
+    loop(1, DP, send_ar, True)
     ar_recv[me] = ar_send[me]
 
     grad_out = jnp.zeros((2 * 32, 2 * HID), jnp.float32)
     for j in range(4):
         cols = slice(1024 * j, 1024 * j + 1024)
-        grad_out += dot(stacked(out_grad[:, cols]), act_two[:, cols], NT)
+        grad_out += dot(stacked(recv2[:, :, cols].reshape(32, 1024)), act_two[:, cols], NT)
     go_send[:, :, 0:HID] = folded(grad_out, 32).reshape(4, 8, HID)
 
     def send_go(i):
@@ -434,45 +414,66 @@
     go_sum[...] = total_out
     go_all[mine] = total_out
 
-    def send_go_all(i):
-        peer = dp_peer(i)
-        to_dp(go_sum, go_all.at[mine], ssem4.at[peer], rsem4.at[me], peer).start()
-
-    loop(1, DP, send_go_all)
     ch_send[2:3, :] = jnp.sum(total_out * total_out, axis=0, keepdims=True)
 
     def arrived_ar(i):
         peer = dp_peer(i)
         to_dp(ar_send.at[peer], ar_recv.at[peer], ssem5.at[peer], rsem5.at[peer], peer).wait_recv()
 
-    loop(1, DP, arrived_ar)
+    loop(1, DP, arrived_ar, True)
     ch_send[0:2, :] = jnp.sum(ar_recv[...], axis=0)
 
     def send_ch(i):
         peer = ch_peer(i)
         to_ch(ch_send, ch_recv.at[col], ssem6.at[peer], rsem6.at[col], peer).start()
 
-    loop(1, CHAN, send_ch)
+    loop(1, CHAN, send_ch, True)
     ch_recv[col] = ch_send[...]
+
+    def send_go_all(i):
+        peer = dp_peer(i)
+        to_dp(go_sum, go_all.at[mine], ssem4.at[peer], rsem4.at[me], peer).start()
+
+    loop(1, DP, send_go_all)
+
+    loop(1, DP, lambda i: sent_dp(i, send1.at[dp_peer(i)], recv1, ssem1, rsem1))
+    for j in range(4):
+        for i in range(1, 4):
+            to_x(i, j).wait_send()
 
     def arrived_ch(i):
         peer = ch_peer(i)
         to_ch(ch_send, ch_recv.at[peer], ssem6.at[peer], rsem6.at[peer], peer).wait_recv()
 
-    loop(1, CHAN, arrived_ch)
+    loop(1, CHAN, arrived_ch, True)
     ag_send[...] = jnp.sum(ch_recv[...], axis=0)
 
     def send_ag(i):
         peer = dp_peer(i)
         to_dp(ag_send, ag_recv.at[me], ssem7.at[peer], rsem7.at[me], peer).start()
 
-    loop(1, DP, send_ag)
+    loop(1, DP, send_ag, True)
     ag_recv[me] = ag_send[...]
 
+    def sent_small(i):
+        n = x_peer(i)
+        to_dp(go_send.at[n], go_recv.at[x], ssem3.at[n], rsem3.at[x], 4 * z + n).wait_send()
+
+    loop(1, 4, sent_small)
+
+    def sent_ch(i):
+        peer = ch_peer(i)
+        to_ch(ch_send, ch_recv.at[col], ssem6.at[peer], rsem6.at[col], peer).wait_send()
+
+    loop(1, CHAN, sent_ch)
+    loop(1, DP, lambda i: sent_dp(i, ar_send.at[dp_peer(i)], ar_recv, ssem5, rsem5))
+    loop(1, DP, lambda i: sent_dp(i, go_sum, go_all, ssem4, rsem4))
+
     def arrived_go_all(i):
         peer = dp_peer(i)
         to_dp(go_sum, go_all.at[peer], ssem4.at[peer], rsem4.at[peer], peer).wait_recv()
 
+    loop(1, DP, lambda i: sent_dp(i, ag_send, ag_recv, ssem7, rsem7))
     loop(1, DP, arrived_go_all)
     full_out = go_all[...].reshape(COLS, 128).T[0:HID, :]
 
@@ -480,7 +481,7 @@
         peer = dp_peer(i)
         to_dp(ag_send, ag_recv.at[peer], ssem7.at[peer], rsem7.at[peer], peer).wait_recv()
 
-    loop(1, DP, arrived_ag)
+    loop(1, DP, arrived_ag, True)
     for i in range(DP):
         pay[2 * i : 2 * i + 2, :] = ag_recv[i, 0:2, :]
     second = pay[0:32, :]
@@ -507,7 +508,18 @@
         line, w_first_ref[0:1, :], m_first_ref[0:1, 0, :], m_first_ref[0:1, 1, :], scale
     )
 
-    sent()
+
+def hand_over(*refs):
+    sources, results, held, sems = refs[:3], refs[3:6], refs[6:9], refs[9]
+    fetch = [pltpu.make_async_copy(sources[n], held[n], sems.at[0, n]) for n in range(3)]
+    write = [pltpu.make_async_copy(held[n], results[n], sems.at[1, n]) for n in range(3)]
+    for copy in fetch:
+        copy.start()
+    for n in range(3):
+        fetch[n].wait()
+        write[n].start()
+    for copy in write:
+        copy.wait()
 
 
 def local(spec_u, spec_g, decay_length, w_first, w_second, w_out, moments_first, moments_second, moments_out):
@@ -520,7 +532,7 @@
     def pair(n):
         return [sem((n,)), sem((n,))]
 
-    return pl.pallas_call(
+    steps = pl.pallas_call(
         kernel,
         out_shape=(
             jax.ShapeDtypeStruct(w_first.shape, f32),
@@ -541,7 +553,7 @@
             vmem((128, 128), f32), vmem((COLS, 128), f32), vmem((HID, 96), bf16), vmem((HID, 192), bf16),
             vmem((96, 4096), bf16), vmem((128, 4096), bf16), vmem((HID, 4096), f32),
             vmem((128, 4096), bf16), vmem((HID, 4096), f32),
-            vmem((4, 8, 4096), f32), vmem((4, 8, 4096), f32), *pair(4),
+            vmem((4, 8, 4096), f32), vmem((4, 8, 4096), f32), sem((4, 4)), sem((4, 4)),
             vmem((4, 8, 128), f32), vmem((4, 8, 128), f32), *pair(4),
             vmem((8, 128), f32), vmem((DP, 8, 128), f32), *pair(DP),
             vmem((64, 128), f32), vmem((DP, 2, 128), f32), vmem((DP, 2, 128), f32), *pair(DP),
@@ -557,6 +569,15 @@
         jnp.swapaxes(moments_first, 0, 1), moments_second, moments_out,
         jnp.asarray(dft_high), jnp.asarray(dft_low), jnp.asarray(last), jnp.asarray(first),
     )
+    return pl.pallas_call(
+        hand_over,
+        out_shape=[jax.ShapeDtypeStruct(step.shape, f32) for step in steps],
+        in_specs=[anywhere] * 3,
+        out_specs=[anywhere] * 3,
+        scratch_shapes=[vmem(step.shape, f32) for step in steps] + [sem((2, 3))],
+        compiler_params=pltpu.CompilerParams(vmem_limit_bytes=56 * 1024 * 1024),
+        name="hand_over",
+    )(*steps)
 
 
 def solution(mesh):

time: 105 us -> 101 us (0.962)
  local copies, waits for them, and re-layouts: 4.18 us -> 0 us
    unnamed x3 -> x0, local copies, waits for them, and re-layouts: 4.18 us -> none
    pallas_call x0 -> x1, Pallas kernels: none -> 1.56 us  [local(): pl.pallas_call(hand_over, out_shape=[jax.ShapeDtypeStruct(step.shape, f32...]
    pallas_call x1, Pallas kernels: 99.9 us -> 98.5 us  [local(): pl.pallas_call(kernel, out_shape=(jax.ShapeDtypeStruct(w_first.shape, f32...]
where the time goes in v4:
time: 101 us
  Pallas kernels  100 us (99%)
    pallas_call x1, Pallas kernels, local(): pl.pallas_call(kernel, out_shape=(jax.ShapeDtypeStruct(w_first.shape, f32...  98.5 us

profile of v4, /device:TPU:1, one launch (start us, length us, event | category | flops | bytes accessed | tf_op | source)
XLA Modules:
  0.0 100.7 jit_solution(8115629882096385869)
XLA Ops:
  0.6 98.5 %hyena_step.1 = (f32[33,64]{1,0:T(8,128)}, f32[64,64]{1,0:T(8,128)}, f32[64,256]{1,0:T(8,128)}) custom-call(f32[2,1024,256]{2,1,0:T(8,128)} %u_hbm.1, f32[2,1024,256]{2,1,0:T(8,128)} %g_hbm.1, f32[1,256]{1,0:T(1,128)} %bitcast.3, f32[33,64]{1,0:T(8,128)} %w_first_hbm.1, f32[64,64]{1,0:T(8,128)} %w_second_hbm.1, f32[64,256]{1,0:T(8,128)} %w_out_hbm.1, ...), custom_call_target="tpu_custom_call" | custom-call | tf_op jit(solution)/shard_map/hyena_step/pallas_call | solution.py:535
  99.2 1.6 %hand_over.1 = (f32[33,64]{1,0:T(8,128)}, f32[64,64]{1,0:T(8,128)}, f32[64,256]{1,0:T(8,128)}) custom-call(f32[33,64]{1,0:T(8,128)} %get-tuple-element.6.refs_0_, f32[64,64]{1,0:T(8,128)} %get-tuple-element.7.refs_1_, f32[64,256]{1,0:T(8,128)} %get-tuple-element.8.refs_2_), custom_call_target="tpu_custom_call" | custom-call | tf_op jit(solution)/shard_map/hand_over/pallas_call | solution.py:572

commit v5 on v4

--- a/solution.py
+++ b/solution.py
@@ -140,8 +140,8 @@
     dft_high_ref, dft_low_ref, last_ref, first_ref, small_sem,
     send1, recv1, ssem1, rsem1,
     mid, x_high, x_low, decay_rows, window,
-    wf, w_rows, w_out_parts, w_second_parts, feats, act_one, cos_one, act_two, cos_two,
-    send2, recv2, ssem2, rsem2,
+    wf, w_rows, w_mine, w_theirs, ssem8, rsem8, w_out_parts, w_second_parts, feats, act_one, cos_one, act_two, cos_two,
+    own2, send2, recv2, ssem2, rsem2,
     go_send, go_recv, ssem3, rsem3,
     go_sum, go_all, ssem4, rsem4,
     pay, ar_send, ar_recv, ssem5, rsem5,
@@ -161,7 +161,8 @@
         return lax.rem(device, 2) * 16 + lax.div(device, 2)
 
     mine = chunk_of(me)
-    z, x = lax.div(me, 4), lax.rem(me, 4)
+    core = lax.rem(col, 2)
+    sibling = col + 1 - 2 * core
 
     def to_dp(src, dst, ssem, rsem, peer):
         return pltpu.make_async_remote_copy(
@@ -253,16 +254,16 @@
     lane = lax.broadcasted_iota(jnp.int32, (8, 128), 1)
 
     def make_window(v):
-        t = 4 * lax.rem(lax.div(v, 8), 4) + lax.div(v, 32) + 16 * lax.rem(v, 8) + 128 * lane
+        t = lax.div(v, 8) + 16 * lax.rem(v, 8) + 128 * lane
         window[pl.ds(pl.multiple_of(v * 8, 8), 8), :] = jnp.exp(-t.astype(jnp.float32) / decay)
 
     loop(0, 128, make_window)
 
     w_rows[:, 0:HID] = w_out_ref[...].T
     w_rows[:, HID:] = jnp.zeros((COLS, 128 - HID), jnp.float32)
-    met = [w_rows[pl.ds(pl.multiple_of(chunk_of(4 * z + n) * 8, 8), 8), :] for n in range(4)]
-    met = jnp.concatenate(met + [jnp.zeros((96, 128), jnp.float32)], axis=0).T
-    w_out_parts[...] = three_lanes(met[0:HID, 0:32])
+    w_mine[...] = w_rows[pl.ds(pl.multiple_of(mine * 8, 8), 8), :]
+    w_copy = to_ch(w_mine, w_theirs, ssem8.at[0], rsem8.at[0], sibling)
+    w_copy.start()
     w_second_parts[...] = three_lanes(w_second_ref[...])
 
     wf[...] = jnp.zeros_like(wf)
@@ -276,7 +277,7 @@
         cols = pl.ds(pl.multiple_of(n * 512, 512), 512)
         column = n * 512 + lax.broadcasted_iota(jnp.int32, (16, 512), 1)
         residue = column >> 7
-        position = 4 * x + (residue >> 3) + 16 * (residue & 7) + 128 * (column & 127)
+        position = 8 * core + (residue >> 3) + 16 * (residue & 7) + 128 * (column & 127)
         band = lax.broadcasted_iota(jnp.int32, (16, 512), 0) + 1
         angle = 2.0 * math.pi / SEQ * ((band * position) & (SEQ - 1)).astype(jnp.float32)
         sine, cosine = sine_cosine(angle)
@@ -292,7 +293,10 @@
         act_two[:, cols] = stacked(sine)
         cos_two[:, cols] = cosine
 
-    loop(0, 8, activations)
+    loop(0, 16, activations)
+    w_copy.wait()
+    met = jnp.concatenate([w_mine[...], w_theirs[...], jnp.zeros((112, 128), jnp.float32)], axis=0).T
+    w_out_parts[...] = three_lanes(met[0:HID, 0:16])
     go_send[...] = jnp.zeros_like(go_send)
     pay[...] = jnp.zeros_like(pay)
     ch_send[...] = jnp.zeros_like(ch_send)
@@ -331,7 +335,7 @@
             s = last_ref[1, v1, v2 : v2 + 1, lanes]
             turned.append((re * c - im * s, re * s + im * c))
         for pair in range(4):
-            rows = pl.ds(pl.multiple_of(lax.rem(v1, 4) * 256 + lax.div(v1, 4) * 64 + pair * 16, 16), 16)
+            rows = pl.ds(pl.multiple_of(v1 * 64 + pair * 16, 16), 16)
             for part, where in ((0, lanes), (1, im_lanes)):
                 x = jnp.concatenate([turned[2 * pair][part], turned[2 * pair + 1][part]], axis=0)
                 high, low = split(x)
@@ -340,38 +344,35 @@
 
     loop(0, 32, pass_two)
 
-    def x_peer(i):
-        return lax.rem(x + i, 4)
-
-    def to_x(i, j):
-        n, cols = x_peer(i), slice(1024 * j, 1024 * j + 1024)
-        return to_dp(send2.at[n, :, cols], recv2.at[x, :, cols], ssem2.at[n, j], rsem2.at[x, j], 4 * z + n)
-
-    def from_x(i, j):
-        n, cols = x_peer(i), slice(1024 * j, 1024 * j + 1024)
-        return to_dp(send2.at[n, :, cols], recv2.at[n, :, cols], ssem2.at[n, j], rsem2.at[n, j], 4 * z + n)
-
-    for j in range(4):
-        rows, cols = slice(256 * j, 256 * j + 256), slice(1024 * j, 1024 * j + 1024)
+    def places(part, half, out):
+        rows = pl.ds(pl.multiple_of(part * 512 + half * 256, 256), 256)
         high, low = x_high[rows, :], x_low[rows, :]
         y = dot(high, dft_high_ref[...], NN) + dot(high, dft_low_ref[...], NN) + dot(low, dft_high_ref[...], NN)
         y = y * window[rows, :]
-        for n in range(4):
-            for v in range(8):
-                row, lanes = 64 * n + 8 * v, 1024 * j + 128 * v
-                send2[n, :, lanes : lanes + 128] = y[row : row + 8, :]
-        for i in (2, 1, 3):
-            to_x(i, j).start()
-        recv2[x, :, cols] = send2[x, :, cols]
+        for v in range(32):
+            lanes = 4096 * half + 128 * v
+            out[:, lanes : lanes + 128] = y[8 * v : 8 * v + 8, :]
+
+    halves = []
+    for half in range(2):
+        places(1 - core, half, send2)
+        cols = slice(4096 * half, 4096 * half + 4096)
+        halves.append(to_ch(send2.at[:, cols], recv2.at[:, cols], ssem2.at[half], rsem2.at[half], sibling))
+        halves[half].start()
+    for half in range(2):
+        places(core, half, own2)
+
+    def met_here(cols):
+        return jnp.concatenate([own2[:, cols], recv2[:, cols]], axis=0)
 
     w_parts, second_parts = w_out_parts[...], w_second_parts[...]
     grad_second = jnp.zeros((2 * HID, 2 * HID), jnp.float32)
     grad_first = jnp.zeros((96, 2 * HID), jnp.float32)
-    for j in range(4):
+    for j in range(8):
         cols = slice(1024 * j, 1024 * j + 1024)
-        for i in (1, 3, 2):
-            from_x(i, j).wait_recv()
-        hidden = dot(w_parts, three_rows(recv2[:, :, cols].reshape(32, 1024)), NN)
+        if j % 4 == 0:
+            halves[j // 4].wait_recv()
+        hidden = dot(w_parts, three_rows(met_here(cols)), NN)
         high, low = split(hidden * cos_two[:, cols])
         grad_second += dot(act_one[:, cols], jnp.concatenate([high, low], axis=0), NT)
         back_one = dot(second_parts, jnp.concatenate([high, low, high], axis=0), NN) * cos_one[:, cols]
@@ -392,25 +393,15 @@
     loop(1, DP, send_ar, True)
     ar_recv[me] = ar_send[me]
 
-    grad_out = jnp.zeros((2 * 32, 2 * HID), jnp.float32)
-    for j in range(4):
+    grad_out = jnp.zeros((2 * 16, 2 * HID), jnp.float32)
+    for j in range(8):
         cols = slice(1024 * j, 1024 * j + 1024)
-        grad_out += dot(stacked(recv2[:, :, cols].reshape(32, 1024)), act_two[:, cols], NT)
-    go_send[:, :, 0:HID] = folded(grad_out, 32).reshape(4, 8, HID)
-
-    def send_go(i):
-        n = x_peer(i)
-        to_dp(go_send.at[n], go_recv.at[x], ssem3.at[n], rsem3.at[x], 4 * z + n).start()
-
-    loop(1, 4, send_go)
-    go_recv[x] = go_send[x]
-
-    def arrived_go(i):
-        n = x_peer(i)
-        to_dp(go_send.at[n], go_recv.at[n], ssem3.at[n], rsem3.at[n], 4 * z + n).wait_recv()
-
-    loop(1, 4, arrived_go)
-    total_out = jnp.sum(go_recv[...], axis=0)
+        grad_out += dot(stacked(met_here(cols)), act_two[:, cols], NT)
+    go_send[:, :, 0:HID] = folded(grad_out, 16).reshape(2, 8, HID)
+    go_copy = to_ch(go_send.at[1], go_recv, ssem3.at[0], rsem3.at[0], sibling)
+    go_copy.start()
+    go_copy.wait()
+    total_out = go_send[0] + go_recv[...]
     go_sum[...] = total_out
     go_all[mine] = total_out
 
@@ -437,9 +428,8 @@
     loop(1, DP, send_go_all)
 
     loop(1, DP, lambda i: sent_dp(i, send1.at[dp_peer(i)], recv1, ssem1, rsem1))
-    for j in range(4):
-        for i in range(1, 4):
-            to_x(i, j).wait_send()
+    for half in range(2):
+        halves[half].wait_send()
 
     def arrived_ch(i):
         peer = ch_peer(i)
@@ -454,12 +444,6 @@
 
     loop(1, DP, send_ag, True)
     ag_recv[me] = ag_send[...]
-
-    def sent_small(i):
-        n = x_peer(i)
-        to_dp(go_send.at[n], go_recv.at[x], ssem3.at[n], rsem3.at[x], 4 * z + n).wait_send()
-
-    loop(1, 4, sent_small)
 
     def sent_ch(i):
         peer = ch_peer(i)
@@ -550,11 +534,12 @@
             vmem((DP, 2, 8, ROWS), f32), vmem((DP, 2, 8, ROWS), f32), *pair(DP),
             vmem((16, 8, 2, 8, 256), f32), vmem((1024, 512), bf16), vmem((1024, 512), bf16),
             vmem((COLS, 128), f32), vmem((1024, 128), f32),
-            vmem((128, 128), f32), vmem((COLS, 128), f32), vmem((HID, 96), bf16), vmem((HID, 192), bf16),
-            vmem((96, 4096), bf16), vmem((128, 4096), bf16), vmem((HID, 4096), f32),
-            vmem((128, 4096), bf16), vmem((HID, 4096), f32),
-            vmem((4, 8, 4096), f32), vmem((4, 8, 4096), f32), sem((4, 4)), sem((4, 4)),
-            vmem((4, 8, 128), f32), vmem((4, 8, 128), f32), *pair(4),
+            vmem((128, 128), f32), vmem((COLS, 128), f32), vmem((8, 128), f32), vmem((8, 128), f32), *pair(1),
+            vmem((HID, 48), bf16), vmem((HID, 192), bf16),
+            vmem((96, 8192), bf16), vmem((128, 8192), bf16), vmem((HID, 8192), f32),
+            vmem((128, 8192), bf16), vmem((HID, 8192), f32),
+            vmem((8, 8192), f32), vmem((8, 8192), f32), vmem((8, 8192), f32), *pair(2),
+            vmem((2, 8, 128), f32), vmem((8, 128), f32), *pair(1),
             vmem((8, 128), f32), vmem((DP, 8, 128), f32), *pair(DP),
             vmem((64, 128), f32), vmem((DP, 2, 128), f32), vmem((DP, 2, 128), f32), *pair(DP),
             vmem((4, 128), f32), vmem((CHAN, 4, 128), f32), *pair(CHAN),

time: 101 us -> 96.5 us (0.955)
  Pallas kernels: 100 us -> 95.6 us
    pallas_call x1, Pallas kernels: 98.5 us -> 94.1 us  [local(): pl.pallas_call(kernel, out_shape=(jax.ShapeDtypeStruct(w_first.shape, f32...]
where the time goes in v5:
time: 96.5 us; the launch traced here: 96.3 us
  Pallas kernels  95.6 us (99%)
    pallas_call x1, Pallas kernels, local(): pl.pallas_call(kernel, out_shape=(jax.ShapeDtypeStruct(w_first.shape, f32...  94.1 us

profile of v5, /device:TPU:1, one launch (start us, length us, event | category | flops | bytes accessed | tf_op | source)
XLA Modules:
  0.0 96.3 jit_solution(7843031733662540218)
XLA Ops:
  0.6 94.1 %hyena_step.1 = (f32[33,64]{1,0:T(8,128)}, f32[64,64]{1,0:T(8,128)}, f32[64,256]{1,0:T(8,128)}) custom-call(f32[2,1024,256]{2,1,0:T(8,128)} %u_hbm.1, f32[2,1024,256]{2,1,0:T(8,128)} %g_hbm.1, f32[1,256]{1,0:T(1,128)} %bitcast.3, f32[33,64]{1,0:T(8,128)} %w_first_hbm.1, f32[64,64]{1,0:T(8,128)} %w_second_hbm.1, f32[64,256]{1,0:T(8,128)} %w_out_hbm.1, ...), custom_call_target="tpu_custom_call" | custom-call | tf_op jit(solution)/shard_map/hyena_step/pallas_call | solution.py:519
  94.7 1.6 %hand_over.1 = (f32[33,64]{1,0:T(8,128)}, f32[64,64]{1,0:T(8,128)}, f32[64,256]{1,0:T(8,128)}) custom-call(f32[33,64]{1,0:T(8,128)} %get-tuple-element.6.refs_0_, f32[64,64]{1,0:T(8,128)} %get-tuple-element.7.refs_1_, f32[64,256]{1,0:T(8,128)} %get-tuple-element.8.refs_2_), custom_call_target="tpu_custom_call" | custom-call | tf_op jit(solution)/shard_map/hand_over/pallas_call | solution.py:557

commit v6 on v5

--- a/solution.py
+++ b/solution.py
@@ -15,7 +15,6 @@
 BANDS = 16
 HID = 64
 DP = 32
-CHAN = 16
 FREQS = 32768
 SEQ = 16384
 ROWS = 1024
@@ -145,7 +144,8 @@
     go_send, go_recv, ssem3, rsem3,
     go_sum, go_all, ssem4, rsem4,
     pay, ar_send, ar_recv, ssem5, rsem5,
-    ch_send, ch_recv, ssem6, rsem6,
+    z_send, z_recv, ssem6, rsem6,
+    y_send, y_recv, ssem9, rsem9,
     ag_send, ag_recv, ssem7, rsem7,
 ):
     me = lax.axis_index("dp")
@@ -154,19 +154,24 @@
     def dp_peer(i):
         return lax.rem(me + i, DP)
 
-    def ch_peer(i):
-        return lax.rem(col + i, CHAN)
-
     def chunk_of(device):
         return lax.rem(device, 2) * 16 + lax.div(device, 2)
 
     mine = chunk_of(me)
-    core = lax.rem(col, 2)
+    z, x = lax.div(me, 4), lax.rem(me, 4)
+    y, core = lax.div(col, 2), lax.rem(col, 2)
+    member = 2 * x + core
     sibling = col + 1 - 2 * core
 
     def to_dp(src, dst, ssem, rsem, peer):
         return pltpu.make_async_remote_copy(
             src_ref=src, dst_ref=dst, send_sem=ssem, recv_sem=rsem, device_id=(peer, col), device_id_type=MESH
+        )
+
+    def to_member(src, dst, ssem, rsem, peer):
+        return pltpu.make_async_remote_copy(
+            src_ref=src, dst_ref=dst, send_sem=ssem, recv_sem=rsem,
+            device_id=(4 * z + lax.div(peer, 2), 2 * y + lax.rem(peer, 2)), device_id_type=MESH,
         )
 
     def to_ch(src, dst, ssem, rsem, peer):
@@ -209,11 +214,16 @@
     def greet_dp(i):
         pl.semaphore_signal(barrier, inc=1, device_id=(dp_peer(i), col), device_id_type=MESH)
 
-    def greet_ch(i):
-        pl.semaphore_signal(barrier, inc=1, device_id=(me, ch_peer(i)), device_id_type=MESH)
-
-    loop(1, DP, greet_dp)
-    loop(1, CHAN, greet_ch)
+    def greet(dp, chan):
+        pl.semaphore_signal(barrier, inc=1, device_id=(dp, chan), device_id_type=MESH)
+
+    for i in sorted(range(1, DP), key=lambda i: -min(i, DP - i)):
+        greet_dp(i)
+    for i in (4, 3, 5, 2, 6, 1, 7):
+        greet(me, 2 * lax.rem(y + i, 8) + core)
+    for i in (2, 1, 3):
+        greet(4 * z + lax.rem(x + i, 4), sibling)
+    greet(me, sibling)
 
     for block in range(2):
         for which in range(2):
@@ -232,7 +242,7 @@
 
         loop(0, ROWS // 128, product)
         if block == 0:
-            pl.semaphore_wait(barrier, DP - 1 + CHAN - 1)
+            pl.semaphore_wait(barrier, DP - 1 + 7 + 4)
 
         def send(i, block=block):
             n = lax.rem(lax.div(me, 2) + i, 16)
@@ -298,14 +308,14 @@
     met = jnp.concatenate([w_mine[...], w_theirs[...], jnp.zeros((112, 128), jnp.float32)], axis=0).T
     w_out_parts[...] = three_lanes(met[0:HID, 0:16])
     go_send[...] = jnp.zeros_like(go_send)
+    ar_send[...] = jnp.zeros_like(ar_send)
     pay[...] = jnp.zeros_like(pay)
-    ch_send[...] = jnp.zeros_like(ch_send)
 
     def arrived1(i):
         peer = dp_peer(i)
         to_dp(send1.at[peer], recv1.at[peer], ssem1.at[peer], rsem1.at[peer], peer).wait_recv()
 
-    loop(1, DP, arrived1)
+    loop(1, DP, arrived1, True)
 
     def pass_one(n):
         q0, lt = lax.div(n, 2), lax.rem(n, 2)
@@ -379,19 +389,52 @@
         grad_first += dot(feats[:, cols], stacked(back_one), NT)
     grad_second = folded(grad_second, HID)
     grad_first = folded(grad_first, 48)
+
     pay[0:32, :] = jnp.concatenate([grad_second[0:32], grad_second[32:64]], axis=1)
     pay[32:48, :] = jnp.concatenate([grad_first[0:16], grad_first[16:32]], axis=1)
     pay[48:49, 0:HID] = grad_first[32:33]
-
-    for i in range(DP):
-        ar_send[i] = pay[2 * i : 2 * i + 2, :]
-
-    def send_ar(i):
-        peer = dp_peer(i)
-        to_dp(ar_send.at[peer], ar_recv.at[me], ssem5.at[peer], rsem5.at[me], peer).start()
-
-    loop(1, DP, send_ar, True)
-    ar_recv[me] = ar_send[me]
+    for i in range(8):
+        ar_send[i, 0:7, :] = pay[7 * i : 7 * i + 7, :]
+
+    def ring(i, at):
+        return lax.rem(at + i, 8)
+
+    def add_copy(i):
+        peer = ring(i, member)
+        return to_member(ar_send.at[peer], ar_recv.at[member], ssem5.at[peer], rsem5.at[member], peer)
+
+    def add_arrival(i):
+        peer = ring(i, member)
+        return to_member(ar_send.at[peer], ar_recv.at[peer], ssem5.at[peer], rsem5.at[peer], peer)
+
+    def z_copy(i):
+        peer = ring(i, z)
+        return to_dp(z_send, z_recv.at[z], ssem6.at[peer], rsem6.at[z], 4 * peer + x)
+
+    def z_arrival(i):
+        peer = ring(i, z)
+        return to_dp(z_send, z_recv.at[peer], ssem6.at[peer], rsem6.at[peer], 4 * peer + x)
+
+    def y_copy(i):
+        peer = ring(i, y)
+        return to_ch(y_send, y_recv.at[y], ssem9.at[peer], rsem9.at[y], 2 * peer + core)
+
+    def y_arrival(i):
+        peer = ring(i, y)
+        return to_ch(y_send, y_recv.at[peer], ssem9.at[peer], rsem9.at[peer], 2 * peer + core)
+
+    def share_copy(i):
+        peer = ring(i, member)
+        return to_member(ag_send, ag_recv.at[member], ssem7.at[peer], rsem7.at[member], peer)
+
+    def share_arrival(i):
+        peer = ring(i, member)
+        return to_member(ag_send, ag_recv.at[peer], ssem7.at[peer], rsem7.at[peer], peer)
+
+    others = (4, 3, 5, 2, 6, 1, 7)
+    for i in others:
+        add_copy(i).start()
+    ar_recv[member] = ar_send[member]
 
     grad_out = jnp.zeros((2 * 16, 2 * HID), jnp.float32)
     for j in range(8):
@@ -405,21 +448,14 @@
     go_sum[...] = total_out
     go_all[mine] = total_out
 
-    ch_send[2:3, :] = jnp.sum(total_out * total_out, axis=0, keepdims=True)
-
-    def arrived_ar(i):
-        peer = dp_peer(i)
-        to_dp(ar_send.at[peer], ar_recv.at[peer], ssem5.at[peer], rsem5.at[peer], peer).wait_recv()
-
-    loop(1, DP, arrived_ar, True)
-    ch_send[0:2, :] = jnp.sum(ar_recv[...], axis=0)
-
-    def send_ch(i):
-        peer = ch_peer(i)
-        to_ch(ch_send, ch_recv.at[col], ssem6.at[peer], rsem6.at[col], peer).start()
-
-    loop(1, CHAN, send_ch, True)
-    ch_recv[col] = ch_send[...]
+
+    for i in others:
+        add_arrival(i).wait_recv()
+    z_send[...] = jnp.sum(ar_recv[...], axis=0)
+    z_send[7:8, :] = jnp.sum(total_out * total_out, axis=0, keepdims=True)
+    for i in others:
+        z_copy(i).start()
+    z_recv[z] = z_send[...]
 
     def send_go_all(i):
         peer = dp_peer(i)
@@ -431,53 +467,45 @@
     for half in range(2):
         halves[half].wait_send()
 
-    def arrived_ch(i):
-        peer = ch_peer(i)
-        to_ch(ch_send, ch_recv.at[peer], ssem6.at[peer], rsem6.at[peer], peer).wait_recv()
-
-    loop(1, CHAN, arrived_ch, True)
-    ag_send[...] = jnp.sum(ch_recv[...], axis=0)
-
-    def send_ag(i):
-        peer = dp_peer(i)
-        to_dp(ag_send, ag_recv.at[me], ssem7.at[peer], rsem7.at[me], peer).start()
-
-    loop(1, DP, send_ag, True)
-    ag_recv[me] = ag_send[...]
-
-    def sent_ch(i):
-        peer = ch_peer(i)
-        to_ch(ch_send, ch_recv.at[col], ssem6.at[peer], rsem6.at[col], peer).wait_send()
-
-    loop(1, CHAN, sent_ch)
-    loop(1, DP, lambda i: sent_dp(i, ar_send.at[dp_peer(i)], ar_recv, ssem5, rsem5))
+    for i in others:
+        z_arrival(i).wait_recv()
+    y_send[...] = jnp.sum(z_recv[...], axis=0)
+    for i in others:
+        y_copy(i).start()
+    y_recv[y] = y_send[...]
+    for i in others:
+        add_copy(i).wait_send()
+        z_copy(i).wait_send()
+    for i in others:
+        y_arrival(i).wait_recv()
+    ag_send[...] = jnp.sum(y_recv[...], axis=0)
+    for i in others:
+        share_copy(i).start()
+    ag_recv[member] = ag_send[...]
+    for i in others:
+        y_copy(i).wait_send()
+        share_copy(i).wait_send()
     loop(1, DP, lambda i: sent_dp(i, go_sum, go_all, ssem4, rsem4))
 
     def arrived_go_all(i):
         peer = dp_peer(i)
         to_dp(go_sum, go_all.at[peer], ssem4.at[peer], rsem4.at[peer], peer).wait_recv()
 
-    loop(1, DP, lambda i: sent_dp(i, ag_send, ag_recv, ssem7, rsem7))
     loop(1, DP, arrived_go_all)
     full_out = go_all[...].reshape(COLS, 128).T[0:HID, :]
 
-    def arrived_ag(i):
-        peer = dp_peer(i)
-        to_dp(ag_send, ag_recv.at[peer], ssem7.at[peer], rsem7.at[peer], peer).wait_recv()
-
-    loop(1, DP, arrived_ag, True)
-    for i in range(DP):
-        pay[2 * i : 2 * i + 2, :] = ag_recv[i, 0:2, :]
+    for i in others:
+        share_arrival(i).wait_recv()
+    blocks = ag_recv[...]
+    squares = jnp.sum(jnp.sum(blocks * blocks, axis=0)[0:7], axis=0, keepdims=True)
+    squares += jnp.sum(blocks, axis=0)[7:8]
+    total = jnp.sum(squares, axis=1, keepdims=True)
+    scale = jnp.minimum(1.0, clip_norm / (jnp.sqrt(total) + 1e-06))
+    for i in range(7):
+        pay[7 * i : 7 * i + 7, :] = ag_recv[i, 0:7, :]
     second = pay[0:32, :]
     first = pay[32:48, :]
     line = pay[48:49, 0:HID]
-    total = (
-        jnp.sum(second * second, keepdims=True)
-        + jnp.sum(first * first, keepdims=True)
-        + jnp.sum(line * line, keepdims=True)
-        + jnp.sum(jnp.sum(ag_recv[:, 2:3, :], axis=0), keepdims=True)
-    )
-    scale = jnp.minimum(1.0, clip_norm / (jnp.sqrt(total) + 1e-06))
     step_out_ref[...] = adam_step(full_out, w_out_ref[...], m_out_ref[0], m_out_ref[1], scale)
     for part in range(2):
         rows, lanes = slice(32 * part, 32 * part + 32), slice(HID * part, HID * part + HID)
@@ -541,9 +569,10 @@
             vmem((8, 8192), f32), vmem((8, 8192), f32), vmem((8, 8192), f32), *pair(2),
             vmem((2, 8, 128), f32), vmem((8, 128), f32), *pair(1),
             vmem((8, 128), f32), vmem((DP, 8, 128), f32), *pair(DP),
-            vmem((64, 128), f32), vmem((DP, 2, 128), f32), vmem((DP, 2, 128), f32), *pair(DP),
-            vmem((4, 128), f32), vmem((CHAN, 4, 128), f32), *pair(CHAN),
-            vmem((4, 128), f32), vmem((DP, 4, 128), f32), *pair(DP),
+            vmem((64, 128), f32), vmem((8, 8, 128), f32), vmem((8, 8, 128), f32), *pair(8),
+            vmem((8, 128), f32), vmem((8, 8, 128), f32), *pair(8),
+            vmem((8, 128), f32), vmem((8, 8, 128), f32), *pair(8),
+            vmem((8, 128), f32), vmem((8, 8, 128), f32), *pair(8),
         ],
         compiler_params=pltpu.CompilerParams(
             collective_id=0, has_side_effects=True, vmem_limit_bytes=56 * 1024 * 1024

time: 96.5 us -> 95.8 us (level)
  no operation moved by 1% of the time
where the time goes in v6:
time: 95.8 us; the launch traced here: 95.6 us
  Pallas kernels  94.9 us (99%)
    pallas_call x1, Pallas kernels, local(): pl.pallas_call(kernel, out_shape=(jax.ShapeDtypeStruct(w_first.shape, f32...  93.4 us

profile of v6, /device:TPU:1, one launch (start us, length us, event | category | flops | bytes accessed | tf_op | source)
XLA Modules:
  0.0 95.6 jit_solution(15261251956196080981)
XLA Ops:
  0.6 93.4 %hyena_step.1 = (f32[33,64]{1,0:T(8,128)}, f32[64,64]{1,0:T(8,128)}, f32[64,256]{1,0:T(8,128)}) custom-call(f32[2,1024,256]{2,1,0:T(8,128)} %u_hbm.1, f32[2,1024,256]{2,1,0:T(8,128)} %g_hbm.1, f32[1,256]{1,0:T(1,128)} %bitcast.3, f32[33,64]{1,0:T(8,128)} %w_first_hbm.1, f32[64,64]{1,0:T(8,128)} %w_second_hbm.1, f32[64,256]{1,0:T(8,128)} %w_out_hbm.1, ...), custom_call_target="tpu_custom_call" | custom-call | tf_op jit(solution)/shard_map/hyena_step/pallas_call | solution.py:547
  94.0 1.6 %hand_over.1 = (f32[33,64]{1,0:T(8,128)}, f32[64,64]{1,0:T(8,128)}, f32[64,256]{1,0:T(8,128)}) custom-call(f32[33,64]{1,0:T(8,128)} %get-tuple-element.6.refs_0_, f32[64,64]{1,0:T(8,128)} %get-tuple-element.7.refs_1_, f32[64,256]{1,0:T(8,128)} %get-tuple-element.8.refs_2_), custom_call_target="tpu_custom_call" | custom-call | tf_op jit(solution)/shard_map/hand_over/pallas_call | solution.py:586

commit v7 on v6

--- a/solution.py
+++ b/solution.py
@@ -127,16 +127,16 @@
     last = (np.stack([np.cos(angle), np.sin(angle)]) / FREQS).astype(np.float32)
     angle = 2.0 * np.pi / 128 * (np.arange(8)[:, None] * np.arange(16)[None, :])
     first = np.stack([np.cos(angle), np.sin(angle)], axis=-1).astype(np.float32)
-    return high, low, last, first.reshape(-1)
+    return np.concatenate([high, low], axis=1), last, first.reshape(-1)
 
 
 def kernel(
     u_hbm, g_hbm, decay_hbm, w_first_hbm, w_second_hbm, w_out_hbm, m_first_hbm, m_second_hbm, m_out_hbm,
-    dft_high_hbm, dft_low_hbm, last_hbm, first_hbm,
+    dft_hbm, last_hbm, first_hbm,
     step_first_ref, step_second_ref, step_out_ref,
     u_buf, g_buf, in_sem,
     decay_ref, w_first_ref, w_second_ref, w_out_ref, m_first_ref, m_second_ref, m_out_ref,
-    dft_high_ref, dft_low_ref, last_ref, first_ref, small_sem,
+    dft_ref, last_ref, first_ref, small_sem,
     send1, recv1, ssem1, rsem1,
     mid, x_high, x_low, decay_rows, window,
     wf, w_rows, w_mine, w_theirs, ssem8, rsem8, w_out_parts, w_second_parts, feats, act_one, cos_one, act_two, cos_two,
@@ -204,7 +204,7 @@
         for n, (src, dst) in enumerate((
             (decay_hbm, decay_ref), (w_first_hbm, w_first_ref), (w_second_hbm, w_second_ref),
             (w_out_hbm, w_out_ref), (m_first_hbm, m_first_ref), (m_second_hbm, m_second_ref),
-            (m_out_hbm, m_out_ref), (dft_high_hbm, dft_high_ref), (dft_low_hbm, dft_low_ref),
+            (m_out_hbm, m_out_ref), (dft_hbm, dft_ref),
             (last_hbm, last_ref), (first_hbm, first_ref),
         ))
     ]
@@ -339,10 +339,10 @@
         im_lanes = pl.ds(pl.multiple_of(256 + lt * 128, 128), 128)
         values = dft([(mid[v1, q0, 0, :, lanes], mid[v1, q0, 1, :, lanes]) for q0 in range(8)])
         turned = []
+        last_cos, last_sin = last_ref[0, v1, :, lanes], last_ref[1, v1, :, lanes]
         for v2 in range(8):
             re, im = values[v2]
-            c = last_ref[0, v1, v2 : v2 + 1, lanes]
-            s = last_ref[1, v1, v2 : v2 + 1, lanes]
+            c, s = last_cos[v2 : v2 + 1], last_sin[v2 : v2 + 1]
             turned.append((re * c - im * s, re * s + im * c))
         for pair in range(4):
             rows = pl.ds(pl.multiple_of(v1 * 64 + pair * 16, 16), 16)
@@ -357,7 +357,8 @@
     def places(part, half, out):
         rows = pl.ds(pl.multiple_of(part * 512 + half * 256, 256), 256)
         high, low = x_high[rows, :], x_low[rows, :]
-        y = dot(high, dft_high_ref[...], NN) + dot(high, dft_low_ref[...], NN) + dot(low, dft_high_ref[...], NN)
+        both = dot(high, dft_ref[...], NN)
+        y = both[:, :128] + both[:, 128:] + dot(low, dft_ref[:, :128], NN)
         y = y * window[rows, :]
         for v in range(32):
             lanes = 4096 * half + 128 * v
@@ -451,11 +452,23 @@
 
     for i in others:
         add_arrival(i).wait_recv()
-    z_send[...] = jnp.sum(ar_recv[...], axis=0)
-    z_send[7:8, :] = jnp.sum(total_out * total_out, axis=0, keepdims=True)
+    out_squares = jnp.sum(total_out * total_out, axis=0, keepdims=True)
+    row = lax.broadcasted_iota(jnp.int32, (8, 128), 0)
+    z_send[...] = jnp.where(row == 7, out_squares, jnp.sum(ar_recv[...], axis=0))
     for i in others:
         z_copy(i).start()
     z_recv[z] = z_send[...]
+
+    loop(1, DP, lambda i: sent_dp(i, send1.at[dp_peer(i)], recv1, ssem1, rsem1))
+    for half in range(2):
+        halves[half].wait_send()
+
+    for i in others:
+        z_arrival(i).wait_recv()
+    y_send[...] = jnp.sum(z_recv[...], axis=0)
+    for i in others:
+        y_copy(i).start()
+    y_recv[y] = y_send[...]
 
     def send_go_all(i):
         peer = dp_peer(i)
@@ -463,16 +476,6 @@
 
     loop(1, DP, send_go_all)
 
-    loop(1, DP, lambda i: sent_dp(i, send1.at[dp_peer(i)], recv1, ssem1, rsem1))
-    for half in range(2):
-        halves[half].wait_send()
-
-    for i in others:
-        z_arrival(i).wait_recv()
-    y_send[...] = jnp.sum(z_recv[...], axis=0)
-    for i in others:
-        y_copy(i).start()
-    y_recv[y] = y_send[...]
     for i in others:
         add_copy(i).wait_send()
         z_copy(i).wait_send()
@@ -535,7 +538,7 @@
 
 
 def local(spec_u, spec_g, decay_length, w_first, w_second, w_out, moments_first, moments_second, moments_out):
-    dft_high, dft_low, last, first = constants()
+    dft_parts, last, first = constants()
     f32, bf16 = jnp.float32, jnp.bfloat16
     vmem, sem = pltpu.VMEM, pltpu.SemaphoreType.DMA
     in_vmem = pl.BlockSpec(memory_space=pltpu.VMEM)
@@ -551,14 +554,13 @@
             jax.ShapeDtypeStruct(w_second.shape, f32),
             jax.ShapeDtypeStruct(w_out.shape, f32),
         ),
-        in_specs=[anywhere] * 13,
+        in_specs=[anywhere] * 12,
         out_specs=(in_vmem,) * 3,
         scratch_shapes=[
             vmem((2, ROWS, COLS), f32), vmem((2, ROWS, COLS), f32), sem((4,)),
             vmem((1, COLS), f32), vmem((33, HID), f32), vmem((HID, HID), f32), vmem((HID, COLS), f32),
             vmem((33, 2, HID), f32), vmem((2, HID, HID), f32), vmem((2, HID, COLS), f32),
-            vmem((512, 128), bf16), vmem((512, 128), bf16), vmem((2, 16, 8, 256), f32),
-            pltpu.SMEM((256,), f32), sem((11,)),
+            vmem((512, 256), bf16), vmem((2, 16, 8, 256), f32), pltpu.SMEM((256,), f32), sem((10,)),
             vmem((DP, 2, 8, ROWS), f32), vmem((DP, 2, 8, ROWS), f32), *pair(DP),
             vmem((16, 8, 2, 8, 256), f32), vmem((1024, 512), bf16), vmem((1024, 512), bf16),
             vmem((COLS, 128), f32), vmem((1024, 128), f32),
@@ -581,7 +583,7 @@
     )(
         spec_u, spec_g, decay_length.reshape(1, COLS), w_first, w_second, w_out,
         jnp.swapaxes(moments_first, 0, 1), moments_second, moments_out,
-        jnp.asarray(dft_high), jnp.asarray(dft_low), jnp.asarray(last), jnp.asarray(first),
+        jnp.asarray(dft_parts), jnp.asarray(last), jnp.asarray(first),
     )
     return pl.pallas_call(
         hand_over,

time: 95.8 us -> 95.6 us (level)
  no operation moved by 1% of the time
where the time goes in v7:
time: 95.6 us; the launch traced here: 95.4 us
  Pallas kernels  94.7 us (99%)
    pallas_call x1, Pallas kernels, local(): pl.pallas_call(kernel, out_shape=(jax.ShapeDtypeStruct(w_first.shape, f32...  93.2 us

profile of v7, /device:TPU:1, one launch (start us, length us, event | category | flops | bytes accessed | tf_op | source)
XLA Modules:
  0.0 95.4 jit_solution(6326968355107550870)
XLA Ops:
  0.6 93.2 %hyena_step.1 = (f32[33,64]{1,0:T(8,128)}, f32[64,64]{1,0:T(8,128)}, f32[64,256]{1,0:T(8,128)}) custom-call(f32[2,1024,256]{2,1,0:T(8,128)} %u_hbm.1, f32[2,1024,256]{2,1,0:T(8,128)} %g_hbm.1, f32[1,256]{1,0:T(1,128)} %bitcast.3, f32[33,64]{1,0:T(8,128)} %w_first_hbm.1, f32[64,64]{1,0:T(8,128)} %w_second_hbm.1, f32[64,256]{1,0:T(8,128)} %w_out_hbm.1, ...), custom_call_target="tpu_custom_call" | custom-call | tf_op jit(solution)/shard_map/hyena_step/pallas_call | solution.py:550
  93.8 1.6 %hand_over.1 = (f32[33,64]{1,0:T(8,128)}, f32[64,64]{1,0:T(8,128)}, f32[64,256]{1,0:T(8,128)}) custom-call(f32[33,64]{1,0:T(8,128)} %get-tuple-element.6.refs_0_, f32[64,64]{1,0:T(8,128)} %get-tuple-element.7.refs_1_, f32[64,256]{1,0:T(8,128)} %get-tuple-element.8.refs_2_), custom_call_target="tpu_custom_call" | custom-call | tf_op jit(solution)/shard_map/hand_over/pallas_call | solution.py:588

commit v8 on v7

--- a/solution.py
+++ b/solution.py
@@ -331,7 +331,11 @@
             mid[v1, q0, 0, :, out_lanes] = re
             mid[v1, q0, 1, :, out_lanes] = im
 
-    loop(0, 16, pass_one)
+    def both_one(n):
+        pass_one(2 * n)
+        pass_one(2 * n + 1)
+
+    loop(0, 8, both_one)
 
     def pass_two(n):
         v1, lt = lax.div(n, 2), lax.rem(n, 2)
@@ -352,7 +356,11 @@
                 x_high[rows, where] = high
                 x_low[rows, where] = low
 
-    loop(0, 32, pass_two)
+    def both_two(n):
+        pass_two(2 * n)
+        pass_two(2 * n + 1)
+
+    loop(0, 16, both_two)
 
     def places(part, half, out):
         rows = pl.ds(pl.multiple_of(part * 512 + half * 256, 256), 256)

time: 95.6 us -> 95.4 us (level)
  no operation moved by 1% of the time
where the time goes in v8:
time: 95.4 us; the launch traced here: 95.2 us
  Pallas kernels  94.5 us (99%)
    pallas_call x1, Pallas kernels, local(): pl.pallas_call(kernel, out_shape=(jax.ShapeDtypeStruct(w_first.shape, f32...  93 us

profile of v8, /device:TPU:1, one launch (start us, length us, event | category | flops | bytes accessed | tf_op | source)
XLA Modules:
  0.0 95.2 jit_solution(10685509174667606136)
XLA Ops:
  0.6 93.0 %hyena_step.1 = (f32[33,64]{1,0:T(8,128)}, f32[64,64]{1,0:T(8,128)}, f32[64,256]{1,0:T(8,128)}) custom-call(f32[2,1024,256]{2,1,0:T(8,128)} %u_hbm.1, f32[2,1024,256]{2,1,0:T(8,128)} %g_hbm.1, f32[1,256]{1,0:T(1,128)} %bitcast.3, f32[33,64]{1,0:T(8,128)} %w_first_hbm.1, f32[64,64]{1,0:T(8,128)} %w_second_hbm.1, f32[64,256]{1,0:T(8,128)} %w_out_hbm.1, ...), custom_call_target="tpu_custom_call" | custom-call | tf_op jit(solution)/shard_map/hyena_step/pallas_call | solution.py:558
  93.6 1.6 %hand_over.1 = (f32[33,64]{1,0:T(8,128)}, f32[64,64]{1,0:T(8,128)}, f32[64,256]{1,0:T(8,128)}) custom-call(f32[33,64]{1,0:T(8,128)} %get-tuple-element.6.refs_0_, f32[64,64]{1,0:T(8,128)} %get-tuple-element.7.refs_1_, f32[64,256]{1,0:T(8,128)} %get-tuple-element.8.refs_2_), custom_call_target="tpu_custom_call" | custom-call | tf_op jit(solution)/shard_map/hand_over/pallas_call | solution.py:596
